TPU v7x, 256 devices: a whole 4x4x8 slice. The times are simulated.
256 devices in a mesh: modes: 32 (over y, z_hi, x), rows: 8 (over z_lo, core).
Axes of the slice: x: 4, y: 4, z: 8 (z_hi: 2, z_lo: 4; z = z_hi * 4 + z_lo), core: 2. Of those that a mesh axis runs over, the one named last changes fastest.
Arguments:
- fwd_fields: bfloat16 [512, 2, 384, 384], P('modes', None, 'rows'), may hold values from -6 to 6
- bwd_fields: bfloat16 [512, 2, 384, 384], P('modes', None, 'rows'), may hold values from -6 to 6
- wavelength: int32 [512], P('modes'), may hold values from 0 to 2
- kernel_phase: float32 [3, 384, 384], replicated, may hold values from -3.140625 to 3.140625
- mask_phase: float32 [384, 384], P('rows'), may hold values from -3.140625 to 3.140625
Outputs:
- fwd_out: bfloat16 [512, 2, 384, 384], P('modes', None, 'rows')
- new_mask: float32 [2, 384, 384], P(None, 'rows')
- coupling: float32 [2, 512], P(None, 'modes')
All inputs are finite; a program needn't handle non-finite values.
Results may differ from a plain program's by a relative error of at most 0.034.
Values may be sent and summed in bfloat16 or wider, within the bound.
No kernel may reach another device: no remote copies, remote signals or barrier semaphores. Data moves between devices by JAX's collectives and lax.ppermute only.
A program may use at most 64 MiB of HBM per device.

v0:
```python
import math

import jax
import jax.numpy as jnp
from jax import lax
from jax.experimental import pallas as pl
from jax.experimental.pallas import tpu as pltpu
from jax.sharding import PartitionSpec as P

N = 384
ROWS = 8
CHIPS = 4
PIECE = N // ROWS
MINE = 2
FIELDS = 512
X_STEPS = (1, 2, 3)
Y_STEPS = (8, 16, 24)
Z_STEP = 4
SMEM = pl.BlockSpec(memory_space=pltpu.SMEM)
VMEM = pl.BlockSpec(memory_space=pltpu.VMEM)
ANY = pl.BlockSpec(memory_space=pl.ANY)
LIMIT = 24 * 1024 * 1024
BF16, F32 = jnp.bfloat16, jnp.float32


def sincos(angle):
    y = angle * 0.5
    z = y * y
    s = -1.0 / 39916800.0
    for c in (1.0 / 362880.0, -1.0 / 5040.0, 1.0 / 120.0, -1.0 / 6.0, 1.0):
        s = s * z + c
    s = s * y
    c = 1.0 / 479001600.0
    for d in (-1.0 / 3628800.0, 1.0 / 40320.0, -1.0 / 720.0, 1.0 / 24.0, -0.5, 1.0):
        c = c * z + d
    return 1.0 - 2.0 * s * s, 2.0 * s * c


def dot(a, b):
    return jnp.dot(a, b, preferred_element_type=F32)


def lanes(i):
    return slice(i * N, (i + 1) * N)


def tables_kernel(row_ref, fields_ref, fore_ref, back_ref, keep_ref, give_ref, one, two):
    for r in range(0, N, 128):
        j = lax.broadcasted_iota(jnp.int32, (128, N), 0) + r
        k = lax.broadcasted_iota(jnp.int32, (128, N), 1)
        jk = (j * k).astype(F32)
        turn = jnp.floor(jk * (1.0 / N) + 0.5)
        cosine, sine = sincos((jk - turn * N) * (2.0 * math.pi / N))
        scale = 1.0 / math.sqrt(N)
        cosine = (cosine * scale).astype(BF16)
        sine = (sine * scale).astype(BF16)
        a, b = pl.ds(r, 128), pl.ds(N + r, 128)
        fore_ref[a, :N] = cosine
        fore_ref[a, N:] = -sine
        fore_ref[b, :N] = sine
        fore_ref[b, N:] = cosine
        back_ref[a, :N] = cosine
        back_ref[a, N:] = sine
        back_ref[b, :N] = -sine
        back_ref[b, N:] = cosine
    for f in range(ROWS * MINE):
        for c in range(2):
            one[f * PIECE : (f + 1) * PIECE, lanes(c)] = fields_ref[f, c]
    for h in range(2):
        two[lanes(h), :] = dot(one[lanes(h), :], fore_ref[...]).astype(BF16)
    for k in range(ROWS):
        out = give_ref if k % 2 else keep_ref
        for f in range(MINE):
            top = pl.multiple_of(((row_ref[0] ^ k) * MINE + f) * PIECE, 16)
            for c in range(2):
                out[k // 2, 2 * f + c] = two[pl.ds(top, PIECE), lanes(c)]


def gate_kernel(row_ref):
    del row_ref


def trig_kernel(row_ref, wave_ref, phase_ref, trig_ref):
    for f in range(MINE):
        wave = wave_ref[row_ref[0] * MINE + f]
        for r in range(0, N, 128):
            cosine, sine = sincos(phase_ref[wave, pl.ds(r, 128), :])
            trig_ref[f, 0, pl.ds(r, 128), :] = cosine
            trig_ref[f, 1, pl.ds(r, 128), :] = sine


def mask_kernel(row_ref, mine_ref, got_ref, mask_ref):
    for k in range(ROWS):
        piece = (got_ref if k % 2 else mine_ref)[k // 2]
        top = pl.multiple_of((row_ref[0] ^ k) * PIECE, 16)
        cosine, sine = sincos(piece.astype(F32))
        mask_ref[0, pl.ds(top, PIECE), :] = cosine
        mask_ref[1, pl.ds(top, PIECE), :] = sine


def spectral(sign, fore_ref, back_ref, trig_ref, one, two):
    for c in range(2):
        one[lanes(c), :] = dot(back_ref[lanes(c), :], two[...]).astype(BF16)
    for f in range(MINE):
        re = one[:N, lanes(f)].astype(F32)
        im = one[N:, lanes(f)].astype(F32)
        cosine, sine = trig_ref[f, 0], sign * trig_ref[f, 1]
        two[:N, lanes(f)] = (cosine * re - sine * im).astype(BF16)
        two[N:, lanes(f)] = (sine * re + cosine * im).astype(BF16)
    for c in range(2):
        d = dot(fore_ref[lanes(c), :], two[...]).astype(BF16)
        for f in range(MINE):
            one[lanes(f), lanes(c)] = d[:, lanes(f)]
    return [dot(one[lanes(f), :], back_ref[...]) for f in range(MINE)]


def block_of(blocks, k):
    if k < 2:
        return blocks[k].at[0]
    return blocks[1 + k // 2].at[pl.ds(k % 2 * 2 * MINE, 2 * MINE)]


def forward_kernel(*refs):
    row_ref, blocks = refs[0], refs[1 : 2 + CHIPS]
    fore_ref, back_ref, trig_ref, space_ref, keep_ref, give_ref, one, two = refs[2 + CHIPS :]
    for k in range(ROWS):
        block = block_of(blocks, k)
        top = pl.multiple_of((row_ref[0] ^ k) * PIECE, 16)
        for f in range(MINE):
            for c in range(2):
                one[pl.ds(f * N + top, PIECE), lanes(c)] = block[2 * f + c]
    for f in range(MINE):
        a = dot(one[lanes(f), :], fore_ref[...]).astype(BF16)
        two[:N, lanes(f)] = a[:, :N]
        two[N:, lanes(f)] = a[:, N:]
    space = spectral(1.0, fore_ref, back_ref, trig_ref, one, two)
    for f in range(MINE):
        space_ref[f] = space[f]
        two[lanes(f), :] = space[f].astype(BF16)
    for k in range(ROWS):
        out = give_ref if k % 2 else keep_ref
        top = pl.multiple_of((row_ref[0] ^ k) * PIECE, 16)
        for f in range(MINE):
            for c in range(2):
                out[k // 2, 2 * f + c] = two[pl.ds(f * N + top, PIECE), lanes(c)]


def total(x):
    return jnp.sum(jnp.sum(x, axis=0, keepdims=True), axis=1, keepdims=True)


def backward_kernel(*refs):
    row_ref, blocks = refs[0], refs[1 : 2 + CHIPS]
    fore_ref, back_ref, trig_ref, space_ref, mask_ref = refs[2 + CHIPS : 7 + CHIPS]
    keep_ref, give_ref, one, two, over = refs[7 + CHIPS :]
    for k in range(ROWS):
        block = block_of(blocks, k)
        top = pl.multiple_of((row_ref[0] ^ k) * PIECE, 16)
        for f in range(MINE):
            for c in range(2):
                two[pl.ds(c * N + top, PIECE), lanes(f)] = block[2 * f + c]
    space = spectral(-1.0, fore_ref, back_ref, trig_ref, one, two)
    cosine, sine = mask_ref[0], mask_ref[1]
    over_re, over_im = 0.0, 0.0
    rows = []
    for f in range(MINE):
        b_re, b_im = space[f][:, :N], space[f][:, N:]
        f_re, f_im = space_ref[f, :, :N], space_ref[f, :, N:]
        g_re = f_re * b_re + f_im * b_im
        g_im = f_im * b_re - f_re * b_im
        c_re = total(g_re * cosine - g_im * sine) * (1.0 / N)
        c_im = total(g_re * sine + g_im * cosine) * (1.0 / N)
        over_re = over_re + (g_re * c_re + g_im * c_im)
        over_im = over_im + (g_im * c_re - g_re * c_im)
        rows += [c_re, c_im]
    scale = 1.0 / math.sqrt(FIELDS)
    over[0] = (over_re * scale).astype(BF16)
    over[1] = (over_im * scale).astype(BF16)
    for k in range(ROWS):
        out = give_ref if k % 2 else keep_ref
        top = pl.multiple_of((row_ref[0] ^ k) * PIECE, 16)
        for c in range(2):
            start = ((k // 2) * 2 + c) * PIECE
            out[start : start + PIECE, :] = over[c, pl.ds(top, PIECE), :]
    high = [r.astype(BF16) for r in rows]
    rest = [r - h.astype(F32) for r, h in zip(rows, high)]
    mid = [r.astype(BF16) for r in rest]
    low = [(r - m.astype(F32)).astype(BF16) for r, m in zip(rest, mid)]
    at = lax.broadcasted_iota(jnp.int32, (16, N), 0)
    packed = jnp.zeros((16, N), F32)
    for t, terms in enumerate((high, mid, low)):
        for i, value in enumerate(terms):
            packed = jnp.where(at == 4 * t + i, value.astype(F32), packed)
    for out in (keep_ref, give_ref):
        out[CHIPS * 2 * PIECE :, :] = packed.astype(BF16)


def core_sum_kernel(keep_ref, got_ref, *outs):
    tail = CHIPS * 2 * PIECE
    for j in range(CHIPS):
        at = slice(j * 2 * PIECE, (j + 1) * 2 * PIECE)
        both = keep_ref[at, :].astype(F32) + got_ref[at, :].astype(F32)
        outs[j][: 2 * PIECE, :] = both.astype(BF16)
        outs[j][2 * PIECE :, :128] = keep_ref[tail:, :128]
        outs[j][2 * PIECE :, 128:256] = got_ref[tail:, 128:256]
        outs[j][2 * PIECE :, 256:] = keep_ref[tail:, 256:]


def four(terms):
    terms = [t.astype(F32) for t in terms]
    return (terms[0] + terms[1]) + (terms[2] + terms[3])


def chip_sum_kernel(at_ref, *refs):
    parts, (over_ref, coup_ref) = refs[:CHIPS], refs[-2:]
    over_ref[...] = four([p[: 2 * PIECE, :] for p in parts]).astype(BF16)
    at = lax.broadcasted_iota(jnp.int32, (1, 128), 1)
    result = [jnp.zeros((1, 128), F32)] * 2
    for k in range(ROWS):
        half = slice(128 * (k % 2), 128 * (k % 2) + 128)
        packed = parts[k // 2][2 * PIECE :, half].astype(F32)
        for f in range(MINE):
            here = at == (at_ref[0] ^ k) * MINE + f
            for c in range(2):
                i = 2 * f + c
                value = packed[i : i + 1] + packed[4 + i : 5 + i] + packed[8 + i : 9 + i]
                result[c] = jnp.where(here, value, result[c])
    coup_ref[...] = jnp.concatenate(result, axis=0)[:, : ROWS * MINE]


def four_sum_kernel(*refs):
    refs[-1][...] = four([r[...] for r in refs[:4]]).astype(BF16)


def final_kernel(row_ref, *refs):
    over_ref, more_ref, *blocks, out_ref, mask_ref = refs
    over = over_ref[...].astype(F32) + more_ref[...].astype(F32)
    re, im = over[:PIECE], over[PIECE:]
    denom = jnp.maximum(jnp.sqrt(re * re + im * im), 1.0)
    re, im = re / denom, im / denom
    mask_ref[0] = re
    mask_ref[1] = im
    for k in range(ROWS):
        block = block_of(blocks, k)
        first = (row_ref[0] ^ k) * MINE
        for f in range(MINE):
            f_re = block[2 * f].astype(F32)
            f_im = block[2 * f + 1].astype(F32)
            out_ref[first + f, 0] = (f_re * re - f_im * im).astype(BF16)
            out_ref[first + f, 1] = (f_re * im + f_im * re).astype(BF16)


def cut_kernel(row_ref, fields_ref, keep_ref, give_ref, sems):
    copies = []
    for k in range(ROWS):
        out = (give_ref if k % 2 else keep_ref).at[k // 2]
        mine = fields_ref.at[pl.ds((row_ref[0] ^ k) * 2 * MINE, 2 * MINE)]
        copies.append(pltpu.make_async_copy(mine, out, sems.at[k]))
    for copy in copies:
        copy.start()
    for copy in copies:
        copy.wait()


def call(kernel, args, outs, scratch=(), flops=0, after=(), places=None, sems=0, through=()):
    args, after = list(args), list(after) + list(through)
    first = len(args) + len(after) - len(through)
    alias = {first + i: len(outs) + i for i in range(len(through))}
    size = sum(a.size * a.dtype.itemsize for a in args) + sum(
        math.prod(s) * jnp.dtype(t).itemsize for s, t in outs
    )
    place = places or VMEM
    scratch_shapes = [pltpu.VMEM(s, t) for s, t in scratch]
    n, m = len(args), len(args) + len(after) + len(outs)

    def body(*refs):
        kernel(*refs[:n], *refs[n + len(after) : m], *refs[m + len(through) :])

    outputs = pl.pallas_call(
        body,
        name=kernel.__name__,
        out_shape=[jax.ShapeDtypeStruct(s, t) for s, t in outs]
        + [jax.ShapeDtypeStruct(t.shape, t.dtype) for t in through],
        in_specs=[SMEM if a.dtype == jnp.int32 else place for a in args] + [ANY] * len(after),
        out_specs=[place] * len(outs) + [ANY] * len(through),
        input_output_aliases=alias,
        scratch_shapes=scratch_shapes + [pltpu.SemaphoreType.DMA((sems,))] * (sems > 0),
        compiler_params=pltpu.CompilerParams(vmem_limit_bytes=LIMIT),
        cost_estimate=pl.CostEstimate(flops=flops, bytes_accessed=size, transcendentals=0),
    )(*args, *after)
    return list(outputs)


def over_rows(block, k, name):
    with jax.named_scope(name):
        return lax.ppermute(block, "rows", [(s, s ^ k) for s in range(ROWS)])


def over_modes(block, k, name):
    with jax.named_scope(name):
        return lax.ppermute(block, "modes", [(s, s ^ k) for s in range(lax.axis_size("modes"))])


def both_cores(keep, give, name, more=()):
    got = over_rows(give, 1, name)
    pairs = [jnp.concatenate([keep[j], got[j], *more]) for j in range(1, CHIPS)]
    return keep, got, pairs


def shards(fwd_fields, bwd_fields, wavelength, kernel_phase, mask_phase):
    at = lax.axis_index("rows").astype(jnp.int32)[None]

    sent = ((CHIPS, 2 * MINE, PIECE, N), BF16)
    low_mask = mask_phase.astype(BF16)[None]
    keep, give = call(
        cut_kernel, [at, fwd_fields.reshape(-1, PIECE, N)], [sent] * 2, places=pl.BlockSpec(memory_space=pltpu.HBM), sems=ROWS
    )
    keep, got, pairs = both_cores(keep, give, "forward_entry_core", [low_mask])
    fwd_blocks = [keep, got] + [
        over_rows(p, 2 * j + 2, f"forward_entry_chip{j + 1}") for j, p in enumerate(pairs)
    ]
    masks = jnp.concatenate([low_mask] + [b[4 * MINE :] for b in fwd_blocks[2:]])
    (mask,) = call(
        mask_kernel, [at, masks, over_rows(masks, 1, "mask_core")], [((2, N, N), F32)]
    )

    wide = (2 * N, 2 * N)
    scratch = [(wide, BF16), (wide, BF16)]
    work = 2 * (2 * N) ** 3
    fore, back, keep, give = call(
        tables_kernel, [at, bwd_fields], [(wide, BF16), (wide, BF16), sent, sent], scratch, work
    )
    got = over_rows(give, 1, "backward_entry_core")
    trig, got = call(
        trig_kernel,
        [at, wavelength, kernel_phase],
        [((MINE, 2, N, N), F32)],
        after=fwd_blocks[2:3],
        through=[got],
    )
    (got,) = call(gate_kernel, [at], [], after=fwd_blocks[3:4], through=[got])
    pairs = [jnp.concatenate([keep[j], got[j]]) for j in range(1, CHIPS)]
    bwd_blocks = [keep, got] + [
        over_rows(p, 2 * j + 2, f"backward_entry_chip{j + 1}") for j, p in enumerate(pairs)
    ]

    space, keep, give = call(
        forward_kernel,
        [at, *fwd_blocks, fore, back, trig],
        [((MINE, N, 2 * N), F32), sent, sent],
        scratch,
        4 * work,
    )
    keep, got, pairs = both_cores(keep, give, "forward_exit_core")
    size = CHIPS * 2 * PIECE + 16
    over_keep, over_give = call(
        backward_kernel,
        [at, *bwd_blocks, fore, back, trig, space, mask],
        [((size, N), BF16), ((size, N), BF16)],
        scratch + [((2, N, N), BF16)],
        3 * work,
    )
    over_got = over_rows(over_give, 1, "over_core")
    sums = call(
        core_sum_kernel,
        [over_keep, over_got],
        [((2 * PIECE + 16, N), BF16)] * CHIPS,
        after=[got],
    )
    parts = [sums[0]] + [over_rows(sums[j], 2 * j, f"over_chip{j}") for j in range(1, CHIPS)]
    small = ((2 * PIECE, N), BF16)
    over, coupling, *pairs = call(
        chip_sum_kernel, [at, *parts], [small, ((2, ROWS * MINE), F32)], through=pairs
    )
    near, far, last = [
        over_rows(p, 2 * j + 2, f"forward_exit_chip{j + 1}") for j, p in enumerate(pairs)
    ]
    terms = [over] + [over_modes(over, k, f"over_x{k}") for k in X_STEPS]
    (over,) = call(four_sum_kernel, terms, [small])
    terms = [over] + [over_modes(over, k, f"over_y{k // 8}") for k in Y_STEPS]
    (over,) = call(four_sum_kernel, terms, [small], after=[far])
    fwd_out, new_mask = call(
        final_kernel,
        [at, over, over_modes(over, Z_STEP, "over_z"), keep, got, near, far, last],
        [((ROWS * MINE, 2, PIECE, N), BF16), ((2, PIECE, N), F32)],
    )
    return fwd_out, new_mask, coupling


def solution(mesh):
    in_specs = (
        P("modes", None, "rows", None),
        P("modes", None, "rows", None),
        P("modes"),
        P(),
        P("rows", None),
    )
    out_specs = (P("modes", None, "rows", None), P(None, "rows", None), P(None, "modes"))
    return jax.shard_map(shards, mesh=mesh, in_specs=in_specs, out_specs=out_specs, check_vma=False)
```

profile of v0, /device:TPU:0, one launch (start us, length us, event | category | flops | bytes accessed | tf_op | source)
XLA Modules:
  0.0 117.9 jit_solution(3764330410119636260)
XLA Ops:
  0.6 0.0 copy-start.1
  0.6 1.3 %copy-done.1 = bf16[16,2,48,384]{3,2,1,0:T(8,128)(2,1)S(1)} copy-done((bf16[16,2,48,384]{3,2,1,0:T(8,128)(2,1)S(1)}, bf16[16,2,48,384]{3,2,1,0:T(8,128)(2,1)}, u32[]{:S(2)}) %copy-start.1) | copy-done | bytes 1179672
  1.9 1.6 %cut_kernel.1 = (bf16[4,4,48,384]{3,2,1,0:T(8,128)(2,1)S(1)}, bf16[4,4,48,384]{3,2,1,0:T(8,128)(2,1)S(1)}) custom-call(s32[1]{0:T(128)} %bitcast.refs_0_, bf16[32,48,384]{2,1,0:T(8,128)(2,1)S(1)} %bitcast.40), custom_call_target="tpu_custom_call" | custom-call | bytes 2359300 | tf_op jit(solution)/shard_map/cut_kernel/pallas_call | solution.py:279
  3.5 0.0 copy-start.4
  3.5 0.1 collective-permute-start
  3.6 2.0 %tables_kernel.1 = (bf16[768,768]{1,0:T(8,128)(2,1)S(1)}, bf16[768,768]{1,0:T(8,128)(2,1)S(1)}, bf16[4,4,48,384]{3,2,1,0:T(8,128)(2,1)S(1)}, bf16[4,4,48,384]{3,2,1,0:T(8,128)(2,1)S(1)}) custom-call(s32[1]{0:T(128)} %bitcast.refs_0_, bf16[16,2,48,384]{3,2,1,0:T(8,128)(2,1)S(1)} %copy-done.3), custom_call_target="tpu_custom_call" | custom-call | flops 905969664 | bytes 4718596 | tf_op jit(solution)/shard_map/tables_kernel/pallas_call | solution.py:279
  5.7 0.6 collective-permute-start.3
  6.3 0.0 collective-permute-done.refs_2_
  6.4 0.0 copy-start
  6.4 0.0 copy-start.2
  6.4 0.2 pad_maximum_fusion
  6.6 0.3 collective-permute-start.2
  6.8 3.3 %collective-permute-start.1 = (bf16[9,48,384]{2,1,0:T(8,128)(2,1)S(1)}, bf16[9,48,384]{2,1,0:T(8,128)(2,1)S(1)}, u32[]{:S(2)}, u32[]{:S(2)}) collective-permute-start(bf16[9,48,384]{2,1,0:T(8,128)(2,1)S(1)} %get-tuple-element.71), channel_id=1, source_target_pairs={{0,4},{1,5},{2,6},{3,7},{4,0},{5,1},{6,2},{7,3},{8,12},{9,13},{10,... | collective-permute-start | bytes 995336 | tf_op jit(solution)/shard_map/forward_entry_chip2/ppermute | solution.py:296
  10.1 1.0 collective-permute-start.7
  11.2 0.0 collective-permute-done.3.refs_4_
  11.2 11.7 %collective-permute-done.2.refs_3_ = bf16[9,48,384]{2,1,0:T(8,128)(2,1)S(1)} collective-permute-done((bf16[9,48,384]{2,1,0:T(8,128)(2,1)S(1)}, bf16[9,48,384]{2,1,0:T(8,128)(2,1)S(1)}, u32[]{:S(2)}, u32[]{:S(2)}) %collective-permute-start.2) | collective-permute-done | bytes 331808 | tf_op jit(solution)/shard_map/forward_entry_chip1/ppermute | solution.py:296
  22.9 1.7 %trig_kernel.1 = (f32[2,2,384,384]{3,2,1,0:T(8,128)S(1)}, bf16[4,4,48,384]{3,2,1,0:T(8,128)(2,1)S(1)}) custom-call(s32[1]{0:T(128)} %bitcast.refs_0_, s32[16]{0:T(128)S(1)} %copy-done.2, f32[3,384,384]{2,1,0:T(8,128)S(1)} %copy-done, bf16[9,48,384]{2,1,0:T(8,128)(2,1)S(1)} %collective-permute-done.2.refs_3_, ...), custom_call_target="tpu_custom_call", output_to_operand_aliasing={{1}: (4, {})} | custom-call | bytes 4128836 | tf_op jit(solution)/shard_map/trig_kernel/pallas_call | solution.py:279
  24.7 8.3 %collective-permute-done.1.refs_1_.refs_4_ = bf16[9,48,384]{2,1,0:T(8,128)(2,1)S(1)} collective-permute-done((bf16[9,48,384]{2,1,0:T(8,128)(2,1)S(1)}, bf16[9,48,384]{2,1,0:T(8,128)(2,1)S(1)}, u32[]{:S(2)}, u32[]{:S(2)}) %collective-permute-start.1) | collective-permute-done | bytes 331808 | tf_op jit(solution)/shard_map/forward_entry_chip2/ppermute | solution.py:296
  33.1 0.1 collective-permute-start.4
  33.2 3.1 %collective-permute-start.5 = (bf16[8,48,384]{2,1,0:T(8,128)(2,1)S(1)}, bf16[8,48,384]{2,1,0:T(8,128)(2,1)S(1)}, u32[]{:S(2)}, u32[]{:S(2)}) collective-permute-start(bf16[8,48,384]{2,1,0:T(8,128)(2,1)S(1)} %pad_maximum_fusion.4), channel_id=1, source_target_pairs={{0,4},{1,5},{2,6},{3,7},{4,0},{5,1},{6,2},{7,3},{8,12},{9,13},{10,... | collective-permute-start | bytes 884744 | tf_op jit(solution)/shard_map/backward_entry_chip2/ppermute | solution.py:296
  36.4 1.4 %collective-permute-start.6 = (bf16[8,48,384]{2,1,0:T(8,128)(2,1)S(1)}, bf16[8,48,384]{2,1,0:T(8,128)(2,1)S(1)}, u32[]{:S(2)}, u32[]{:S(2)}) collective-permute-start(bf16[8,48,384]{2,1,0:T(8,128)(2,1)S(1)} %pad_maximum_fusion.5), channel_id=1, source_target_pairs={{0,6},{1,7},{2,4},{3,5},{4,2},{5,3},{6,0},{7,1},{8,14},{9,15},{10,... | collective-permute-start | bytes 884744 | tf_op jit(solution)/shard_map/backward_entry_chip3/ppermute | solution.py:296
  37.8 0.0 collective-permute-done.7.refs_5_
  37.8 4.5 %forward_kernel.1 = (f32[2,384,768]{2,1,0:T(8,128)S(1)}, bf16[4,4,48,384]{3,2,1,0:T(8,128)(2,1)S(1)}, bf16[4,4,48,384]{3,2,1,0:T(8,128)(2,1)S(1)}) custom-call(s32[1]{0:T(128)} %bitcast.refs_0_, bf16[4,4,48,384]{3,2,1,0:T(8,128)(2,1)S(1)} %get-tuple-element.28.refs_1_, bf16[4,4,48,384]{3,2,1,0:T(8,128)(2,1)S(1)} %collective-permute-done.refs_2_, ...), custom_call_target="tpu_custom_call" | custom-call | flops 3623878656 | bytes 10432516 | tf_op jit(solution)/shard_map/forward_kernel/pallas_call | solution.py:279
  42.4 0.3 collective-permute-start.10
  42.7 0.6 collective-permute-start.8
  43.3 1.5 %collective-permute-done.8.refs_2_ = bf16[4,48,384]{2,1,0:T(8,128)(2,1)S(1)} collective-permute-done((bf16[4,48,384]{2,1,0:T(8,128)(2,1)S(1)}, bf16[4,48,384]{2,1,0:T(8,128)(2,1)S(1)}, u32[]{:S(2)}, u32[]{:S(2)}) %collective-permute-start.8) | collective-permute-done | bytes 147488 | tf_op jit(solution)/shard_map/mask_core/ppermute | solution.py:296
  44.8 0.6 mask_kernel.1.refs_10_
  45.4 0.0 collective-permute-done.4.refs_3_
  45.5 13.6 %collective-permute-done.5.refs_4_ = bf16[8,48,384]{2,1,0:T(8,128)(2,1)S(1)} collective-permute-done((bf16[8,48,384]{2,1,0:T(8,128)(2,1)S(1)}, bf16[8,48,384]{2,1,0:T(8,128)(2,1)S(1)}, u32[]{:S(2)}, u32[]{:S(2)}) %collective-permute-start.5) | collective-permute-done | bytes 294944 | tf_op jit(solution)/shard_map/backward_entry_chip2/ppermute | solution.py:296
  59.1 0.0 collective-permute-done.6.refs_5_
  59.1 4.6 %backward_kernel.1 = (bf16[400,384]{1,0:T(8,128)(2,1)S(1)}, bf16[400,384]{1,0:T(8,128)(2,1)S(1)}) custom-call(s32[1]{0:T(128)} %bitcast.refs_0_, bf16[4,4,48,384]{3,2,1,0:T(8,128)(2,1)S(1)} %get-tuple-element.27.refs_1_, bf16[4,4,48,384]{3,2,1,0:T(8,128)(2,1)S(1)} %gate_kernel.1.refs_2_, bf16[8,48,384]{2,1,0:T(8,128)(2,1)S(1)} %collective-permute-done.4.refs_3_, ...), custom_call_target="tpu_custom_call" | custom-call | flops 2717908992 | bytes 10936324 | tf_op jit(solution)/shard_map/backward_kernel/pallas_call | solution.py:279
  63.7 0.1 collective-permute-start.9
  63.8 0.0 collective-permute-done.10.refs_2_.refs_4_
  63.8 0.1 pad_maximum_fusion.6
  63.9 1.4 %collective-permute-done.9.refs_1_ = bf16[400,384]{1,0:T(8,128)(2,1)S(1)} collective-permute-done((bf16[400,384]{1,0:T(8,128)(2,1)S(1)}, bf16[400,384]{1,0:T(8,128)(2,1)S(1)}, u32[]{:S(2)}, u32[]{:S(2)}) %collective-permute-start.9) | collective-permute-done | bytes 307232 | tf_op jit(solution)/shard_map/over_core/ppermute | solution.py:296
  65.4 0.1 core_sum_kernel.1
  65.4 6.0 %collective-permute-start.11 = (bf16[112,384]{1,0:T(8,128)(2,1)S(1)}, bf16[112,384]{1,0:T(8,128)(2,1)S(1)}, u32[]{:S(2)}, u32[]{:S(2)}) collective-permute-start(bf16[112,384]{1,0:T(8,128)(2,1)S(1)} %get-tuple-element.40), channel_id=1, source_target_pairs={{0,2},{1,3},{2,0},{3,1},{4,6},{5,7},{6,4},{7,5},{8,10},{9,11},{10,... | collective-permute-start | bytes 258056 | tf_op jit(solution)/shard_map/over_chip1/ppermute | solution.py:296
  71.5 1.1 collective-permute-start.12
  72.6 1.4 %collective-permute-start.13 = (bf16[112,384]{1,0:T(8,128)(2,1)S(1)}, bf16[112,384]{1,0:T(8,128)(2,1)S(1)}, u32[]{:S(2)}, u32[]{:S(2)}) collective-permute-start(bf16[112,384]{1,0:T(8,128)(2,1)S(1)} %get-tuple-element.42), channel_id=1, source_target_pairs={{0,6},{1,7},{2,4},{3,5},{4,2},{5,3},{6,0},{7,1},{8,14},{9,15},{10,... | collective-permute-start | bytes 258056 | tf_op jit(solution)/shard_map/over_chip3/ppermute | solution.py:296
  74.0 0.3 collective-permute-done.11.refs_2_
  74.3 6.9 %collective-permute-done.12.refs_3_ = bf16[112,384]{1,0:T(8,128)(2,1)S(1)} collective-permute-done((bf16[112,384]{1,0:T(8,128)(2,1)S(1)}, bf16[112,384]{1,0:T(8,128)(2,1)S(1)}, u32[]{:S(2)}, u32[]{:S(2)}) %collective-permute-start.12) | collective-permute-done | bytes 86048 | tf_op jit(solution)/shard_map/over_chip2/ppermute | solution.py:296
  81.3 0.0 collective-permute-done.13.refs_4_
  81.3 0.6 chip_sum_kernel.1
  81.9 1.5 %collective-permute-start.14 = (bf16[96,384]{1,0:T(8,128)(2,1)S(1)}, bf16[96,384]{1,0:T(8,128)(2,1)S(1)}, u32[]{:S(2)}, u32[]{:S(2)}) collective-permute-start(bf16[96,384]{1,0:T(8,128)(2,1)S(1)} %get-tuple-element.44.refs_0_), channel_id=1, source_target_pairs={{0,8},{8,0},{16,24},{24,16},{32,40},{40,32},{48,56},{56,48},{64,72... | collective-permute-start | bytes 221192 | tf_op jit(solution)/shard_map/over_x1/ppermute | solution.py:301
  83.3 2.4 %collective-permute-start.20 = (bf16[8,48,384]{2,1,0:T(8,128)(2,1)S(1)}, bf16[8,48,384]{2,1,0:T(8,128)(2,1)S(1)}, u32[]{:S(2)}, u32[]{:S(2)}) collective-permute-start(bf16[8,48,384]{2,1,0:T(8,128)(2,1)S(1)} %get-tuple-element.45), channel_id=1, source_target_pairs={{0,4},{1,5},{2,6},{3,7},{4,0},{5,1},{6,2},{7,3},{8,12},{9,13},{10,... | collective-permute-start | bytes 884744 | tf_op jit(solution)/shard_map/forward_exit_chip2/ppermute | solution.py:296
  85.8 2.7 %collective-permute-start.15 = (bf16[96,384]{1,0:T(8,128)(2,1)S(1)}, bf16[96,384]{1,0:T(8,128)(2,1)S(1)}, u32[]{:S(2)}, u32[]{:S(2)}) collective-permute-start(bf16[96,384]{1,0:T(8,128)(2,1)S(1)} %get-tuple-element.44.refs_0_), channel_id=1, source_target_pairs={{0,16},{8,24},{16,0},{24,8},{32,48},{40,56},{48,32},{56,40},{64,80... | collective-permute-start | bytes 221192 | tf_op jit(solution)/shard_map/over_x2/ppermute | solution.py:301
  88.5 0.5 collective-permute-start.16
  89.0 0.2 collective-permute-start.22
  89.2 0.0 collective-permute-done.14.refs_1_
  89.2 1.8 %collective-permute-start.23 = (bf16[8,48,384]{2,1,0:T(8,128)(2,1)S(1)}, bf16[8,48,384]{2,1,0:T(8,128)(2,1)S(1)}, u32[]{:S(2)}, u32[]{:S(2)}) collective-permute-start(bf16[8,48,384]{2,1,0:T(8,128)(2,1)S(1)} %get-tuple-element.47), channel_id=1, source_target_pairs={{0,6},{1,7},{2,4},{3,5},{4,2},{5,3},{6,0},{7,1},{8,14},{9,15},{10,... | collective-permute-start | bytes 884744 | tf_op jit(solution)/shard_map/forward_exit_chip3/ppermute | solution.py:296
  90.9 0.7 collective-permute-done.15.refs_2_
  91.7 2.4 %collective-permute-done.16.refs_3_ = bf16[96,384]{1,0:T(8,128)(2,1)S(1)} collective-permute-done((bf16[96,384]{1,0:T(8,128)(2,1)S(1)}, bf16[96,384]{1,0:T(8,128)(2,1)S(1)}, u32[]{:S(2)}, u32[]{:S(2)}) %collective-permute-start.16) | collective-permute-done | bytes 73760 | tf_op jit(solution)/shard_map/over_x3/ppermute | solution.py:301
  94.1 1.7 %collective-permute-start.17 = (bf16[96,384]{1,0:T(8,128)(2,1)S(1)}, bf16[96,384]{1,0:T(8,128)(2,1)S(1)}, u32[]{:S(2)}, u32[]{:S(2)}) collective-permute-start(bf16[96,384]{1,0:T(8,128)(2,1)S(1)} %four_sum_kernel.2.refs_0_), channel_id=1, source_target_pairs={{0,64},{8,72},{16,80},{24,88},{32,96},{40,104},{48,112},{56,120},{... | collective-permute-start | bytes 221192 | tf_op jit(solution)/shard_map/over_y1/ppermute | solution.py:301
  95.8 2.9 %collective-permute-start.18 = (bf16[96,384]{1,0:T(8,128)(2,1)S(1)}, bf16[96,384]{1,0:T(8,128)(2,1)S(1)}, u32[]{:S(2)}, u32[]{:S(2)}) collective-permute-start(bf16[96,384]{1,0:T(8,128)(2,1)S(1)} %four_sum_kernel.2.refs_0_), channel_id=1, source_target_pairs={{0,128},{8,136},{16,144},{24,152},{32,160},{40,168},{48,176},{56,1... | collective-permute-start | bytes 221192 | tf_op jit(solution)/shard_map/over_y2/ppermute | solution.py:301
  98.7 0.3 collective-permute-done.17.refs_1_
  99.0 2.6 %collective-permute-start.19 = (bf16[96,384]{1,0:T(8,128)(2,1)S(1)}, bf16[96,384]{1,0:T(8,128)(2,1)S(1)}, u32[]{:S(2)}, u32[]{:S(2)}) collective-permute-start(bf16[96,384]{1,0:T(8,128)(2,1)S(1)} %four_sum_kernel.2.refs_0_), channel_id=1, source_target_pairs={{0,192},{8,200},{16,208},{24,216},{32,224},{40,232},{48,240},{56,2... | collective-permute-start | bytes 221192 | tf_op jit(solution)/shard_map/over_y3/ppermute | solution.py:301
  101.6 0.3 collective-permute-done.18.refs_2_
  101.8 2.7 %collective-permute-done.19.refs_3_ = bf16[96,384]{1,0:T(8,128)(2,1)S(1)} collective-permute-done((bf16[96,384]{1,0:T(8,128)(2,1)S(1)}, bf16[96,384]{1,0:T(8,128)(2,1)S(1)}, u32[]{:S(2)}, u32[]{:S(2)}) %collective-permute-start.19) | collective-permute-done | bytes 73760 | tf_op jit(solution)/shard_map/over_y3/ppermute | solution.py:301
  104.5 1.5 %collective-permute-done.20.refs_4_.refs_6_ = bf16[8,48,384]{2,1,0:T(8,128)(2,1)S(1)} collective-permute-done((bf16[8,48,384]{2,1,0:T(8,128)(2,1)S(1)}, bf16[8,48,384]{2,1,0:T(8,128)(2,1)S(1)}, u32[]{:S(2)}, u32[]{:S(2)}) %collective-permute-start.20) | collective-permute-done | bytes 294944 | tf_op jit(solution)/shard_map/forward_exit_chip2/ppermute | solution.py:296
  106.1 7.1 %collective-permute-start.21 = (bf16[96,384]{1,0:T(8,128)(2,1)S(1)}, bf16[96,384]{1,0:T(8,128)(2,1)S(1)}, u32[]{:S(2)}, u32[]{:S(2)}) collective-permute-start(bf16[96,384]{1,0:T(8,128)(2,1)S(1)} %four_sum_kernel.3.refs_1_), channel_id=1, source_target_pairs={{0,32},{8,40},{16,48},{24,56},{32,0},{40,8},{48,16},{56,24},{64,96... | collective-permute-start | bytes 221192 | tf_op jit(solution)/shard_map/over_z/ppermute | solution.py:301
  113.2 0.0 collective-permute-done.22.refs_5_
  113.2 0.0 collective-permute-done.23.refs_7_
  113.2 3.2 %collective-permute-done.21.refs_2_ = bf16[96,384]{1,0:T(8,128)(2,1)S(1)} collective-permute-done((bf16[96,384]{1,0:T(8,128)(2,1)S(1)}, bf16[96,384]{1,0:T(8,128)(2,1)S(1)}, u32[]{:S(2)}, u32[]{:S(2)}) %collective-permute-start.21) | collective-permute-done | bytes 73760 | tf_op jit(solution)/shard_map/over_z/ppermute | solution.py:301
  116.4 1.5 %final_kernel.1 = (bf16[16,2,48,384]{3,2,1,0:T(8,128)(2,1)}, f32[2,48,384]{2,1,0:T(8,128)}) custom-call(s32[1]{0:T(128)} %bitcast.refs_0_, bf16[96,384]{1,0:T(8,128)(2,1)S(1)} %four_sum_kernel.3.refs_1_, bf16[96,384]{1,0:T(8,128)(2,1)S(1)} %collective-permute-done.21.refs_2_, bf16[4,4,48,384]{3,2,1,0:T(8,128)(2,1)S(1)} %get-tuple-element.43.refs_3_, ...), custom_call_target="tpu_custom_call" | custom-call | bytes 3538948 | tf_op jit(solution)/shard_map/final_kernel/pallas_call | solution.py:279
  (23 shorter events, 0.6 us)
Async XLA Ops:
  0.6 1.3 %copy-start.1 = (bf16[16,2,48,384]{3,2,1,0:T(8,128)(2,1)S(1)}, bf16[16,2,48,384]{3,2,1,0:T(8,128)(2,1)}, u32[]{:S(2)}) copy-start(bf16[16,2,48,384]{3,2,1,0:T(8,128)(2,1)} %param.5) | copy-start | bytes 3538948
  1.9 1.7 %copy-start.3 = (bf16[16,2,48,384]{3,2,1,0:T(8,128)(2,1)S(1)}, bf16[16,2,48,384]{3,2,1,0:T(8,128)(2,1)}, u32[]{:S(2)}) copy-start(bf16[16,2,48,384]{3,2,1,0:T(8,128)(2,1)} %refs_1_.2) | copy-start | bytes 3538948
  3.5 2.7 %copy-start.4 = (f32[48,384]{1,0:T(8,128)S(1)}, f32[48,384]{1,0:T(8,128)}, u32[]{:S(2)}) copy-start(f32[48,384]{1,0:T(8,128)} %param.9) | copy-start | bytes 221188
  3.5 2.8 %collective-permute-start = (bf16[4,4,48,384]{3,2,1,0:T(8,128)(2,1)S(1)}, bf16[4,4,48,384]{3,2,1,0:T(8,128)(2,1)S(1)}, u32[]{:S(2)}, u32[]{:S(2)}) collective-permute-start(bf16[4,4,48,384]{3,2,1,0:T(8,128)(2,1)S(1)} %get-tuple-element.29), channel_id=1, source_target_pairs={{0,1},{1,0},{2,3},{3,2},{4,5},{5,4},{6,7},{7,6},{8,9},{9,8},{10,11... | collective-permute-start | bytes 1769480 | tf_op jit(solution)/shard_map/forward_entry_core/ppermute | solution.py:296
  5.7 5.5 %collective-permute-start.3 = (bf16[4,4,48,384]{3,2,1,0:T(8,128)(2,1)S(1)}, bf16[4,4,48,384]{3,2,1,0:T(8,128)(2,1)S(1)}, u32[]{:S(2)}, u32[]{:S(2)}) collective-permute-start(bf16[4,4,48,384]{3,2,1,0:T(8,128)(2,1)S(1)} %get-tuple-element.30), channel_id=1, source_target_pairs={{0,1},{1,0},{2,3},{3,2},{4,5},{5,4},{6,7},{7,6},{8,9},{9,8},{10,11... | collective-permute-start | bytes 1769480 | tf_op jit(solution)/shard_map/backward_entry_core/ppermute | solution.py:296
  6.4 16.6 %copy-start = (f32[3,384,384]{2,1,0:T(8,128)S(1)}, f32[3,384,384]{2,1,0:T(8,128)}, u32[]{:S(2)}) copy-start(f32[3,384,384]{2,1,0:T(8,128)} %refs_2_.1) | copy-start | bytes 5308420
  6.4 16.5 %copy-start.2 = (s32[16]{0:T(128)S(1)}, s32[16]{0:T(128)}, u32[]{:S(2)}) copy-start(s32[16]{0:T(128)} %refs_1_.3) | copy-start | bytes 196
  6.6 16.4 %collective-permute-start.2 = (bf16[9,48,384]{2,1,0:T(8,128)(2,1)S(1)}, bf16[9,48,384]{2,1,0:T(8,128)(2,1)S(1)}, u32[]{:S(2)}, u32[]{:S(2)}) collective-permute-start(bf16[9,48,384]{2,1,0:T(8,128)(2,1)S(1)} %get-tuple-element.70), channel_id=1, source_target_pairs={{0,2},{1,3},{2,0},{3,1},{4,6},{5,7},{6,4},{7,5},{8,10},{9,11},{10,... | collective-permute-start | bytes 995336 | tf_op jit(solution)/shard_map/forward_entry_chip1/ppermute | solution.py:296
  6.8 26.2 %collective-permute-start.1 = (bf16[9,48,384]{2,1,0:T(8,128)(2,1)S(1)}, bf16[9,48,384]{2,1,0:T(8,128)(2,1)S(1)}, u32[]{:S(2)}, u32[]{:S(2)}) collective-permute-start(bf16[9,48,384]{2,1,0:T(8,128)(2,1)S(1)} %get-tuple-element.71), channel_id=1, source_target_pairs={{0,4},{1,5},{2,6},{3,7},{4,0},{5,1},{6,2},{7,3},{8,12},{9,13},{10,... | collective-permute-start | bytes 995336 | tf_op jit(solution)/shard_map/forward_entry_chip2/ppermute | solution.py:296
  10.1 27.7 %collective-permute-start.7 = (bf16[9,48,384]{2,1,0:T(8,128)(2,1)S(1)}, bf16[9,48,384]{2,1,0:T(8,128)(2,1)S(1)}, u32[]{:S(2)}, u32[]{:S(2)}) collective-permute-start(bf16[9,48,384]{2,1,0:T(8,128)(2,1)S(1)} %get-tuple-element.69), channel_id=1, source_target_pairs={{0,6},{1,7},{2,4},{3,5},{4,2},{5,3},{6,0},{7,1},{8,14},{9,15},{10,... | collective-permute-start | bytes 995336 | tf_op jit(solution)/shard_map/forward_entry_chip3/ppermute | solution.py:296
  33.1 12.4 %collective-permute-start.4 = (bf16[8,48,384]{2,1,0:T(8,128)(2,1)S(1)}, bf16[8,48,384]{2,1,0:T(8,128)(2,1)S(1)}, u32[]{:S(2)}, u32[]{:S(2)}) collective-permute-start(bf16[8,48,384]{2,1,0:T(8,128)(2,1)S(1)} %pad_maximum_fusion.3), channel_id=1, source_target_pairs={{0,2},{1,3},{2,0},{3,1},{4,6},{5,7},{6,4},{7,5},{8,10},{9,11},{10,... | collective-permute-start | bytes 884744 | tf_op jit(solution)/shard_map/backward_entry_chip1/ppermute | solution.py:296
  33.2 25.8 %collective-permute-start.5 = (bf16[8,48,384]{2,1,0:T(8,128)(2,1)S(1)}, bf16[8,48,384]{2,1,0:T(8,128)(2,1)S(1)}, u32[]{:S(2)}, u32[]{:S(2)}) collective-permute-start(bf16[8,48,384]{2,1,0:T(8,128)(2,1)S(1)} %pad_maximum_fusion.4), channel_id=1, source_target_pairs={{0,4},{1,5},{2,6},{3,7},{4,0},{5,1},{6,2},{7,3},{8,12},{9,13},{10,... | collective-permute-start | bytes 884744 | tf_op jit(solution)/shard_map/backward_entry_chip2/ppermute | solution.py:296
  36.4 22.7 %collective-permute-start.6 = (bf16[8,48,384]{2,1,0:T(8,128)(2,1)S(1)}, bf16[8,48,384]{2,1,0:T(8,128)(2,1)S(1)}, u32[]{:S(2)}, u32[]{:S(2)}) collective-permute-start(bf16[8,48,384]{2,1,0:T(8,128)(2,1)S(1)} %pad_maximum_fusion.5), channel_id=1, source_target_pairs={{0,6},{1,7},{2,4},{3,5},{4,2},{5,3},{6,0},{7,1},{8,14},{9,15},{10,... | collective-permute-start | bytes 884744 | tf_op jit(solution)/shard_map/backward_entry_chip3/ppermute | solution.py:296
  42.4 21.4 %collective-permute-start.10 = (bf16[4,4,48,384]{3,2,1,0:T(8,128)(2,1)S(1)}, bf16[4,4,48,384]{3,2,1,0:T(8,128)(2,1)S(1)}, u32[]{:S(2)}, u32[]{:S(2)}) collective-permute-start(bf16[4,4,48,384]{3,2,1,0:T(8,128)(2,1)S(1)} %get-tuple-element.38), channel_id=1, source_target_pairs={{0,1},{1,0},{2,3},{3,2},{4,5},{5,4},{6,7},{7,6},{8,9},{9,8},{10,11... | collective-permute-start | bytes 1769480 | tf_op jit(solution)/shard_map/forward_exit_core/ppermute | solution.py:296
  42.7 2.1 %collective-permute-start.8 = (bf16[4,48,384]{2,1,0:T(8,128)(2,1)S(1)}, bf16[4,48,384]{2,1,0:T(8,128)(2,1)S(1)}, u32[]{:S(2)}, u32[]{:S(2)}) collective-permute-start(bf16[4,48,384]{2,1,0:T(8,128)(2,1)S(1)} %pad_maximum_fusion.9.refs_1_), channel_id=1, source_target_pairs={{0,1},{1,0},{2,3},{3,2},{4,5},{5,4},{6,7},{7,6},{8,9},{9,8},{10,11... | collective-permute-start | bytes 442376 | tf_op jit(solution)/shard_map/mask_core/ppermute | solution.py:296
  63.7 1.7 %collective-permute-start.9 = (bf16[400,384]{1,0:T(8,128)(2,1)S(1)}, bf16[400,384]{1,0:T(8,128)(2,1)S(1)}, u32[]{:S(2)}, u32[]{:S(2)}) collective-permute-start(bf16[400,384]{1,0:T(8,128)(2,1)S(1)} %get-tuple-element.37), channel_id=1, source_target_pairs={{0,1},{1,0},{2,3},{3,2},{4,5},{5,4},{6,7},{7,6},{8,9},{9,8},{10,11... | collective-permute-start | bytes 921608 | tf_op jit(solution)/shard_map/over_core/ppermute | solution.py:296
  65.4 8.9 %collective-permute-start.11 = (bf16[112,384]{1,0:T(8,128)(2,1)S(1)}, bf16[112,384]{1,0:T(8,128)(2,1)S(1)}, u32[]{:S(2)}, u32[]{:S(2)}) collective-permute-start(bf16[112,384]{1,0:T(8,128)(2,1)S(1)} %get-tuple-element.40), channel_id=1, source_target_pairs={{0,2},{1,3},{2,0},{3,1},{4,6},{5,7},{6,4},{7,5},{8,10},{9,11},{10,... | collective-permute-start | bytes 258056 | tf_op jit(solution)/shard_map/over_chip1/ppermute | solution.py:296
  71.5 9.8 %collective-permute-start.12 = (bf16[112,384]{1,0:T(8,128)(2,1)S(1)}, bf16[112,384]{1,0:T(8,128)(2,1)S(1)}, u32[]{:S(2)}, u32[]{:S(2)}) collective-permute-start(bf16[112,384]{1,0:T(8,128)(2,1)S(1)} %get-tuple-element.41), channel_id=1, source_target_pairs={{0,4},{1,5},{2,6},{3,7},{4,0},{5,1},{6,2},{7,3},{8,12},{9,13},{10,... | collective-permute-start | bytes 258056 | tf_op jit(solution)/shard_map/over_chip2/ppermute | solution.py:296
  72.6 8.7 %collective-permute-start.13 = (bf16[112,384]{1,0:T(8,128)(2,1)S(1)}, bf16[112,384]{1,0:T(8,128)(2,1)S(1)}, u32[]{:S(2)}, u32[]{:S(2)}) collective-permute-start(bf16[112,384]{1,0:T(8,128)(2,1)S(1)} %get-tuple-element.42), channel_id=1, source_target_pairs={{0,6},{1,7},{2,4},{3,5},{4,2},{5,3},{6,0},{7,1},{8,14},{9,15},{10,... | collective-permute-start | bytes 258056 | tf_op jit(solution)/shard_map/over_chip3/ppermute | solution.py:296
  81.9 7.3 %collective-permute-start.14 = (bf16[96,384]{1,0:T(8,128)(2,1)S(1)}, bf16[96,384]{1,0:T(8,128)(2,1)S(1)}, u32[]{:S(2)}, u32[]{:S(2)}) collective-permute-start(bf16[96,384]{1,0:T(8,128)(2,1)S(1)} %get-tuple-element.44.refs_0_), channel_id=1, source_target_pairs={{0,8},{8,0},{16,24},{24,16},{32,40},{40,32},{48,56},{56,48},{64,72... | collective-permute-start | bytes 221192 | tf_op jit(solution)/shard_map/over_x1/ppermute | solution.py:301
  83.3 22.7 %collective-permute-start.20 = (bf16[8,48,384]{2,1,0:T(8,128)(2,1)S(1)}, bf16[8,48,384]{2,1,0:T(8,128)(2,1)S(1)}, u32[]{:S(2)}, u32[]{:S(2)}) collective-permute-start(bf16[8,48,384]{2,1,0:T(8,128)(2,1)S(1)} %get-tuple-element.45), channel_id=1, source_target_pairs={{0,4},{1,5},{2,6},{3,7},{4,0},{5,1},{6,2},{7,3},{8,12},{9,13},{10,... | collective-permute-start | bytes 884744 | tf_op jit(solution)/shard_map/forward_exit_chip2/ppermute | solution.py:296
  85.8 5.9 %collective-permute-start.15 = (bf16[96,384]{1,0:T(8,128)(2,1)S(1)}, bf16[96,384]{1,0:T(8,128)(2,1)S(1)}, u32[]{:S(2)}, u32[]{:S(2)}) collective-permute-start(bf16[96,384]{1,0:T(8,128)(2,1)S(1)} %get-tuple-element.44.refs_0_), channel_id=1, source_target_pairs={{0,16},{8,24},{16,0},{24,8},{32,48},{40,56},{48,32},{56,40},{64,80... | collective-permute-start | bytes 221192 | tf_op jit(solution)/shard_map/over_x2/ppermute | solution.py:301
  88.5 5.6 %collective-permute-start.16 = (bf16[96,384]{1,0:T(8,128)(2,1)S(1)}, bf16[96,384]{1,0:T(8,128)(2,1)S(1)}, u32[]{:S(2)}, u32[]{:S(2)}) collective-permute-start(bf16[96,384]{1,0:T(8,128)(2,1)S(1)} %get-tuple-element.44.refs_0_), channel_id=1, source_target_pairs={{0,24},{8,16},{16,8},{24,0},{32,56},{40,48},{48,40},{56,32},{64,88... | collective-permute-start | bytes 221192 | tf_op jit(solution)/shard_map/over_x3/ppermute | solution.py:301
  89.0 24.2 %collective-permute-start.22 = (bf16[8,48,384]{2,1,0:T(8,128)(2,1)S(1)}, bf16[8,48,384]{2,1,0:T(8,128)(2,1)S(1)}, u32[]{:S(2)}, u32[]{:S(2)}) collective-permute-start(bf16[8,48,384]{2,1,0:T(8,128)(2,1)S(1)} %get-tuple-element.46), channel_id=1, source_target_pairs={{0,2},{1,3},{2,0},{3,1},{4,6},{5,7},{6,4},{7,5},{8,10},{9,11},{10,... | collective-permute-start | bytes 884744 | tf_op jit(solution)/shard_map/forward_exit_chip1/ppermute | solution.py:296
  89.2 24.0 %collective-permute-start.23 = (bf16[8,48,384]{2,1,0:T(8,128)(2,1)S(1)}, bf16[8,48,384]{2,1,0:T(8,128)(2,1)S(1)}, u32[]{:S(2)}, u32[]{:S(2)}) collective-permute-start(bf16[8,48,384]{2,1,0:T(8,128)(2,1)S(1)} %get-tuple-element.47), channel_id=1, source_target_pairs={{0,6},{1,7},{2,4},{3,5},{4,2},{5,3},{6,0},{7,1},{8,14},{9,15},{10,... | collective-permute-start | bytes 884744 | tf_op jit(solution)/shard_map/forward_exit_chip3/ppermute | solution.py:296
  94.1 4.9 %collective-permute-start.17 = (bf16[96,384]{1,0:T(8,128)(2,1)S(1)}, bf16[96,384]{1,0:T(8,128)(2,1)S(1)}, u32[]{:S(2)}, u32[]{:S(2)}) collective-permute-start(bf16[96,384]{1,0:T(8,128)(2,1)S(1)} %four_sum_kernel.2.refs_0_), channel_id=1, source_target_pairs={{0,64},{8,72},{16,80},{24,88},{32,96},{40,104},{48,112},{56,120},{... | collective-permute-start | bytes 221192 | tf_op jit(solution)/shard_map/over_y1/ppermute | solution.py:301
  95.8 6.0 %collective-permute-start.18 = (bf16[96,384]{1,0:T(8,128)(2,1)S(1)}, bf16[96,384]{1,0:T(8,128)(2,1)S(1)}, u32[]{:S(2)}, u32[]{:S(2)}) collective-permute-start(bf16[96,384]{1,0:T(8,128)(2,1)S(1)} %four_sum_kernel.2.refs_0_), channel_id=1, source_target_pairs={{0,128},{8,136},{16,144},{24,152},{32,160},{40,168},{48,176},{56,1... | collective-permute-start | bytes 221192 | tf_op jit(solution)/shard_map/over_y2/ppermute | solution.py:301
  99.0 5.6 %collective-permute-start.19 = (bf16[96,384]{1,0:T(8,128)(2,1)S(1)}, bf16[96,384]{1,0:T(8,128)(2,1)S(1)}, u32[]{:S(2)}, u32[]{:S(2)}) collective-permute-start(bf16[96,384]{1,0:T(8,128)(2,1)S(1)} %four_sum_kernel.2.refs_0_), channel_id=1, source_target_pairs={{0,192},{8,200},{16,208},{24,216},{32,224},{40,232},{48,240},{56,2... | collective-permute-start | bytes 221192 | tf_op jit(solution)/shard_map/over_y3/ppermute | solution.py:301
  106.1 10.3 %collective-permute-start.21 = (bf16[96,384]{1,0:T(8,128)(2,1)S(1)}, bf16[96,384]{1,0:T(8,128)(2,1)S(1)}, u32[]{:S(2)}, u32[]{:S(2)}) collective-permute-start(bf16[96,384]{1,0:T(8,128)(2,1)S(1)} %four_sum_kernel.3.refs_1_), channel_id=1, source_target_pairs={{0,32},{8,40},{16,48},{24,56},{32,0},{40,8},{48,16},{56,24},{64,96... | collective-permute-start | bytes 221192 | tf_op jit(solution)/shard_map/over_z/ppermute | solution.py:301
where the time goes:
time: 120 us; the launch traced here: 118 us
  waiting for transfers between devices  55.1 us (46%)
  starting transfers between devices  42.6 us (36%)
  Pallas kernels  17.3 us (14%)
  local copies, waits for them, and re-layouts  1.58 us (1%)
    ppermute x17, waiting for transfers between devices, over_rows(): return lax.ppermute(block, 'rows', [(s, s ^ k) for s in range(ROWS)])  45.4 us
    ppermute x17, starting transfers between devices, over_rows(): return lax.ppermute(block, 'rows', [(s, s ^ k) for s in range(ROWS)])  23.7 us
    ppermute x7, starting transfers between devices, over_modes(): lax.ppermute(block, 'modes', [(s, s ^ k) for s in range(lax.axis_size('mo...  18.9 us
    pallas_call x12, Pallas kernels, call(): pl.pallas_call(body, name=kernel.__name__, out_shape=[jax.ShapeDtypeStruc...  17.3 us
    ppermute x7, waiting for transfers between devices, over_modes(): lax.ppermute(block, 'modes', [(s, s ^ k) for s in range(lax.axis_size('mo...  9.64 us
  transfers between devices with their start and end apart: 24, of which 14 were waited for; matrix products, arithmetic and copies ran while one was open for 1% of the time, Pallas kernels for 12%

commit v1 on v0

--- a/solution.py
+++ b/solution.py
@@ -250,27 +250,19 @@
             out_ref[first + f, 1] = (f_re * im + f_im * re).astype(BF16)
 
 
-def cut_kernel(row_ref, fields_ref, keep_ref, give_ref, sems):
-    copies = []
-    for k in range(ROWS):
-        out = (give_ref if k % 2 else keep_ref).at[k // 2]
-        mine = fields_ref.at[pl.ds((row_ref[0] ^ k) * 2 * MINE, 2 * MINE)]
-        copies.append(pltpu.make_async_copy(mine, out, sems.at[k]))
-    for copy in copies:
-        copy.start()
-    for copy in copies:
-        copy.wait()
-
-
-def call(kernel, args, outs, scratch=(), flops=0, after=(), places=None, sems=0, through=()):
+def cut_kernel(row_ref, fields_ref, keep_ref, give_ref):
+    for k in range(ROWS):
+        out = give_ref if k % 2 else keep_ref
+        out[k // 2] = fields_ref[pl.ds((row_ref[0] ^ k) * 2 * MINE, 2 * MINE)]
+
+
+def call(kernel, args, outs, scratch=(), flops=0, after=(), through=()):
     args, after = list(args), list(after) + list(through)
     first = len(args) + len(after) - len(through)
     alias = {first + i: len(outs) + i for i in range(len(through))}
     size = sum(a.size * a.dtype.itemsize for a in args) + sum(
         math.prod(s) * jnp.dtype(t).itemsize for s, t in outs
     )
-    place = places or VMEM
-    scratch_shapes = [pltpu.VMEM(s, t) for s, t in scratch]
     n, m = len(args), len(args) + len(after) + len(outs)
 
     def body(*refs):
@@ -281,10 +273,10 @@
         name=kernel.__name__,
         out_shape=[jax.ShapeDtypeStruct(s, t) for s, t in outs]
         + [jax.ShapeDtypeStruct(t.shape, t.dtype) for t in through],
-        in_specs=[SMEM if a.dtype == jnp.int32 else place for a in args] + [ANY] * len(after),
-        out_specs=[place] * len(outs) + [ANY] * len(through),
+        in_specs=[SMEM if a.dtype == jnp.int32 else VMEM for a in args] + [ANY] * len(after),
+        out_specs=[VMEM] * len(outs) + [ANY] * len(through),
         input_output_aliases=alias,
-        scratch_shapes=scratch_shapes + [pltpu.SemaphoreType.DMA((sems,))] * (sems > 0),
+        scratch_shapes=[pltpu.VMEM(s, t) for s, t in scratch],
         compiler_params=pltpu.CompilerParams(vmem_limit_bytes=LIMIT),
         cost_estimate=pl.CostEstimate(flops=flops, bytes_accessed=size, transcendentals=0),
     )(*args, *after)
@@ -312,9 +304,7 @@
 
     sent = ((CHIPS, 2 * MINE, PIECE, N), BF16)
     low_mask = mask_phase.astype(BF16)[None]
-    keep, give = call(
-        cut_kernel, [at, fwd_fields.reshape(-1, PIECE, N)], [sent] * 2, places=pl.BlockSpec(memory_space=pltpu.HBM), sems=ROWS
-    )
+    keep, give = call(cut_kernel, [at, fwd_fields.reshape(-1, PIECE, N)], [sent] * 2)
     keep, got, pairs = both_cores(keep, give, "forward_entry_core", [low_mask])
     fwd_blocks = [keep, got] + [
         over_rows(p, 2 * j + 2, f"forward_entry_chip{j + 1}") for j, p in enumerate(pairs)
@@ -352,6 +342,7 @@
         4 * work,
     )
     keep, got, pairs = both_cores(keep, give, "forward_exit_core")
+    start1, pairs[1] = over_rows(keep[2], 4, "forward_exit_start2"), got[2]
     size = CHIPS * 2 * PIECE + 16
     over_keep, over_give = call(
         backward_kernel,
@@ -370,11 +361,17 @@
     parts = [sums[0]] + [over_rows(sums[j], 2 * j, f"over_chip{j}") for j in range(1, CHIPS)]
     small = ((2 * PIECE, N), BF16)
     over, coupling, *pairs = call(
-        chip_sum_kernel, [at, *parts], [small, ((2, ROWS * MINE), F32)], through=pairs
+        chip_sum_kernel,
+        [at, *parts],
+        [small, ((2, ROWS * MINE), F32)],
+        after=[start1],
+        through=pairs,
+
     )
     near, far, last = [
         over_rows(p, 2 * j + 2, f"forward_exit_chip{j + 1}") for j, p in enumerate(pairs)
     ]
+    far = jnp.concatenate([start1, far])
     terms = [over] + [over_modes(over, k, f"over_x{k}") for k in X_STEPS]
     (over,) = call(four_sum_kernel, terms, [small])
     terms = [over] + [over_modes(over, k, f"over_y{k // 8}") for k in Y_STEPS]

time: 120 us -> 117 us (0.975); the launches traced: 118 us -> 117 us
  Pallas kernels: 17.3 us -> 15.9 us
    ppermute x7, starting transfers between devices: 18.9 us -> 15.3 us  [over_modes(): lax.ppermute(block, 'modes', [(s, s ^ k) for s in range(lax.axis_size('mo...]
    ppermute x17 -> x18, starting transfers between devices: 23.7 us -> 26.9 us  [over_rows(): return lax.ppermute(block, 'rows', [(s, s ^ k) for s in range(ROWS)])]
    ppermute x17 -> x18, waiting for transfers between devices: 45.4 us -> 43.9 us  [over_rows(): return lax.ppermute(block, 'rows', [(s, s ^ k) for s in range(ROWS)])]
    pallas_call x12, Pallas kernels: 17.3 us -> 15.9 us  [call(): pl.pallas_call(body, name=kernel.__name__, out_shape=[jax.ShapeDtypeStruc...]
    ppermute x7, waiting for transfers between devices: 9.64 us -> 11 us  [over_modes(): lax.ppermute(block, 'modes', [(s, s ^ k) for s in range(lax.axis_size('mo...]
  transfers between devices with their start and end apart: 24 -> 25, of which waited for: 14 -> 11; matrix products, arithmetic and copies ran while one was open for 1% -> 1% of each run, Pallas kernels for 12% -> 12%
where the time goes in v1:
time: 117 us
  waiting for transfers between devices  54.9 us (47%)
  starting transfers between devices  42.2 us (36%)
  Pallas kernels  15.9 us (14%)
  local copies, waits for them, and re-layouts  2.67 us (2%)
    ppermute x18, waiting for transfers between devices, over_rows(): return lax.ppermute(block, 'rows', [(s, s ^ k) for s in range(ROWS)])  43.9 us
    ppermute x18, starting transfers between devices, over_rows(): return lax.ppermute(block, 'rows', [(s, s ^ k) for s in range(ROWS)])  26.9 us
    pallas_call x12, Pallas kernels, call(): pl.pallas_call(body, name=kernel.__name__, out_shape=[jax.ShapeDtypeStruc...  15.9 us
    ppermute x7, starting transfers between devices, over_modes(): lax.ppermute(block, 'modes', [(s, s ^ k) for s in range(lax.axis_size('mo...  15.3 us
    ppermute x7, waiting for transfers between devices, over_modes(): lax.ppermute(block, 'modes', [(s, s ^ k) for s in range(lax.axis_size('mo...  11 us
    unnamed x11, local copies, waits for them, and re-layouts  2.35 us
  transfers between devices with their start and end apart: 25, of which 11 were waited for; matrix products, arithmetic and copies ran while one was open for 1% of the time, Pallas kernels for 12%

profile of v1, /device:TPU:0, one launch (start us, length us, event | category | flops | bytes accessed | tf_op | source)
XLA Modules:
  0.0 116.9 jit_solution(17832997349310958611)
XLA Ops:
  0.6 1.3 %copy-done.1 = bf16[16,2,48,384]{3,2,1,0:T(8,128)(2,1)S(1)} copy-done((bf16[16,2,48,384]{3,2,1,0:T(8,128)(2,1)S(1)}, bf16[16,2,48,384]{3,2,1,0:T(8,128)(2,1)}, u32[]{:S(2)}) %copy-start.1) | copy-done | bytes 1179672
  1.9 0.1 cut_kernel.1
  2.0 0.0 copy-start.4
  2.0 0.1 collective-permute-start
  2.1 1.1 copy-done.3
  3.2 2.0 %tables_kernel.1 = (bf16[768,768]{1,0:T(8,128)(2,1)S(1)}, bf16[768,768]{1,0:T(8,128)(2,1)S(1)}, bf16[4,4,48,384]{3,2,1,0:T(8,128)(2,1)S(1)}, bf16[4,4,48,384]{3,2,1,0:T(8,128)(2,1)S(1)}) custom-call(s32[1]{0:T(128)} %bitcast.refs_0_, bf16[16,2,48,384]{3,2,1,0:T(8,128)(2,1)S(1)} %copy-done.3), custom_call_target="tpu_custom_call" | custom-call | flops 905969664 | bytes 4718596 | tf_op jit(solution)/shard_map/tables_kernel/pallas_call | solution.py:271
  5.2 0.1 collective-permute-start.3
  5.4 0.0 collective-permute-done.refs_2_
  5.5 0.0 copy-start
  5.5 0.0 copy-start.2
  5.5 0.2 pad_maximum_fusion
  5.6 0.3 collective-permute-start.2
  5.9 3.3 %collective-permute-start.1 = (bf16[9,48,384]{2,1,0:T(8,128)(2,1)S(1)}, bf16[9,48,384]{2,1,0:T(8,128)(2,1)S(1)}, u32[]{:S(2)}, u32[]{:S(2)}) collective-permute-start(bf16[9,48,384]{2,1,0:T(8,128)(2,1)S(1)} %get-tuple-element.71), channel_id=1, source_target_pairs={{0,4},{1,5},{2,6},{3,7},{4,0},{5,1},{6,2},{7,3},{8,12},{9,13},{10,... | collective-permute-start | bytes 995336 | tf_op jit(solution)/shard_map/forward_entry_chip2/ppermute | solution.py:288
  9.2 1.0 collective-permute-start.7
  10.3 0.0 collective-permute-done.3.refs_4_
  10.3 12.5 %collective-permute-done.2.refs_3_ = bf16[9,48,384]{2,1,0:T(8,128)(2,1)S(1)} collective-permute-done((bf16[9,48,384]{2,1,0:T(8,128)(2,1)S(1)}, bf16[9,48,384]{2,1,0:T(8,128)(2,1)S(1)}, u32[]{:S(2)}, u32[]{:S(2)}) %collective-permute-start.2) | collective-permute-done | bytes 331808 | tf_op jit(solution)/shard_map/forward_entry_chip1/ppermute | solution.py:288
  22.7 1.7 %trig_kernel.1 = (f32[2,2,384,384]{3,2,1,0:T(8,128)S(1)}, bf16[4,4,48,384]{3,2,1,0:T(8,128)(2,1)S(1)}) custom-call(s32[1]{0:T(128)} %bitcast.refs_0_, s32[16]{0:T(128)S(1)} %copy-done.2, f32[3,384,384]{2,1,0:T(8,128)S(1)} %copy-done, bf16[9,48,384]{2,1,0:T(8,128)(2,1)S(1)} %collective-permute-done.2.refs_3_, ...), custom_call_target="tpu_custom_call", output_to_operand_aliasing={{1}: (4, {})} | custom-call | bytes 4128836 | tf_op jit(solution)/shard_map/trig_kernel/pallas_call | solution.py:271
  24.5 7.6 %collective-permute-done.1.refs_1_.refs_4_ = bf16[9,48,384]{2,1,0:T(8,128)(2,1)S(1)} collective-permute-done((bf16[9,48,384]{2,1,0:T(8,128)(2,1)S(1)}, bf16[9,48,384]{2,1,0:T(8,128)(2,1)S(1)}, u32[]{:S(2)}, u32[]{:S(2)}) %collective-permute-start.1) | collective-permute-done | bytes 331808 | tf_op jit(solution)/shard_map/forward_entry_chip2/ppermute | solution.py:288
  32.1 0.1 collective-permute-start.4
  32.3 3.1 %collective-permute-start.5 = (bf16[8,48,384]{2,1,0:T(8,128)(2,1)S(1)}, bf16[8,48,384]{2,1,0:T(8,128)(2,1)S(1)}, u32[]{:S(2)}, u32[]{:S(2)}) collective-permute-start(bf16[8,48,384]{2,1,0:T(8,128)(2,1)S(1)} %pad_maximum_fusion.4), channel_id=1, source_target_pairs={{0,4},{1,5},{2,6},{3,7},{4,0},{5,1},{6,2},{7,3},{8,12},{9,13},{10,... | collective-permute-start | bytes 884744 | tf_op jit(solution)/shard_map/backward_entry_chip2/ppermute | solution.py:288
  35.4 1.4 %collective-permute-start.6 = (bf16[8,48,384]{2,1,0:T(8,128)(2,1)S(1)}, bf16[8,48,384]{2,1,0:T(8,128)(2,1)S(1)}, u32[]{:S(2)}, u32[]{:S(2)}) collective-permute-start(bf16[8,48,384]{2,1,0:T(8,128)(2,1)S(1)} %pad_maximum_fusion.5), channel_id=1, source_target_pairs={{0,6},{1,7},{2,4},{3,5},{4,2},{5,3},{6,0},{7,1},{8,14},{9,15},{10,... | collective-permute-start | bytes 884744 | tf_op jit(solution)/shard_map/backward_entry_chip3/ppermute | solution.py:288
  36.9 0.0 collective-permute-done.7.refs_5_
  36.9 0.3 collective-permute-start.8
  37.2 4.5 %forward_kernel.1 = (f32[2,384,768]{2,1,0:T(8,128)S(1)}, bf16[4,4,48,384]{3,2,1,0:T(8,128)(2,1)S(1)}, bf16[4,4,48,384]{3,2,1,0:T(8,128)(2,1)S(1)}) custom-call(s32[1]{0:T(128)} %bitcast.refs_0_, bf16[4,4,48,384]{3,2,1,0:T(8,128)(2,1)S(1)} %get-tuple-element.28.refs_1_, bf16[4,4,48,384]{3,2,1,0:T(8,128)(2,1)S(1)} %collective-permute-done.refs_2_, ...), custom_call_target="tpu_custom_call" | custom-call | flops 3623878656 | bytes 10432516 | tf_op jit(solution)/shard_map/forward_kernel/pallas_call | solution.py:271
  41.8 0.6 collective-permute-start.10
  42.3 0.0 collective-permute-done.8.refs_2_
  42.3 0.6 mask_kernel.1.refs_10_
  42.9 0.0 collective-permute-done.4.refs_3_
  42.9 15.2 %collective-permute-done.5.refs_4_ = bf16[8,48,384]{2,1,0:T(8,128)(2,1)S(1)} collective-permute-done((bf16[8,48,384]{2,1,0:T(8,128)(2,1)S(1)}, bf16[8,48,384]{2,1,0:T(8,128)(2,1)S(1)}, u32[]{:S(2)}, u32[]{:S(2)}) %collective-permute-start.5) | collective-permute-done | bytes 294944 | tf_op jit(solution)/shard_map/backward_entry_chip2/ppermute | solution.py:288
  58.1 4.6 %backward_kernel.1 = (bf16[400,384]{1,0:T(8,128)(2,1)S(1)}, bf16[400,384]{1,0:T(8,128)(2,1)S(1)}) custom-call(s32[1]{0:T(128)} %bitcast.refs_0_, bf16[4,4,48,384]{3,2,1,0:T(8,128)(2,1)S(1)} %get-tuple-element.27.refs_1_, bf16[4,4,48,384]{3,2,1,0:T(8,128)(2,1)S(1)} %gate_kernel.1.refs_2_, bf16[8,48,384]{2,1,0:T(8,128)(2,1)S(1)} %collective-permute-done.4.refs_3_, ...), custom_call_target="tpu_custom_call" | custom-call | flops 2717908992 | bytes 10936324 | tf_op jit(solution)/shard_map/backward_kernel/pallas_call | solution.py:271
  62.7 0.1 collective-permute-start.9
  62.9 7.6 %collective-permute-start.14 = (bf16[4,48,384]{2,1,0:T(8,128)(2,1)S(1)}, bf16[4,48,384]{2,1,0:T(8,128)(2,1)S(1)}, u32[]{:S(2)}, u32[]{:S(2)}) collective-permute-start(bf16[4,48,384]{2,1,0:T(8,128)(2,1)S(1)} %get-tuple-element.53), channel_id=1, source_target_pairs={{0,4},{1,5},{2,6},{3,7},{4,0},{5,1},{6,2},{7,3},{8,12},{9,13},{10,... | collective-permute-start | bytes 442376 | tf_op jit(solution)/shard_map/forward_exit_start2/ppermute | solution.py:288
  70.5 0.0 collective-permute-done.9.refs_1_
  70.5 0.1 core_sum_kernel.1
  70.6 0.5 collective-permute-start.11
  71.0 1.5 %collective-permute-start.12 = (bf16[112,384]{1,0:T(8,128)(2,1)S(1)}, bf16[112,384]{1,0:T(8,128)(2,1)S(1)}, u32[]{:S(2)}, u32[]{:S(2)}) collective-permute-start(bf16[112,384]{1,0:T(8,128)(2,1)S(1)} %get-tuple-element.41), channel_id=1, source_target_pairs={{0,4},{1,5},{2,6},{3,7},{4,0},{5,1},{6,2},{7,3},{8,12},{9,13},{10,... | collective-permute-start | bytes 258056 | tf_op jit(solution)/shard_map/over_chip2/ppermute | solution.py:288
  72.6 2.5 %collective-permute-start.13 = (bf16[112,384]{1,0:T(8,128)(2,1)S(1)}, bf16[112,384]{1,0:T(8,128)(2,1)S(1)}, u32[]{:S(2)}, u32[]{:S(2)}) collective-permute-start(bf16[112,384]{1,0:T(8,128)(2,1)S(1)} %get-tuple-element.42), channel_id=1, source_target_pairs={{0,6},{1,7},{2,4},{3,5},{4,2},{5,3},{6,0},{7,1},{8,14},{9,15},{10,... | collective-permute-start | bytes 258056 | tf_op jit(solution)/shard_map/over_chip3/ppermute | solution.py:288
  75.0 0.1 pad_maximum_fusion.6
  75.1 6.9 %collective-permute-done.14.refs_5_ = bf16[4,48,384]{2,1,0:T(8,128)(2,1)S(1)} collective-permute-done((bf16[4,48,384]{2,1,0:T(8,128)(2,1)S(1)}, bf16[4,48,384]{2,1,0:T(8,128)(2,1)S(1)}, u32[]{:S(2)}, u32[]{:S(2)}) %collective-permute-start.14) | collective-permute-done | bytes 147488 | tf_op jit(solution)/shard_map/forward_exit_start2/ppermute | solution.py:288
  82.0 0.0 collective-permute-done.11.refs_2_
  82.0 1.8 %collective-permute-done.12.refs_3_ = bf16[112,384]{1,0:T(8,128)(2,1)S(1)} collective-permute-done((bf16[112,384]{1,0:T(8,128)(2,1)S(1)}, bf16[112,384]{1,0:T(8,128)(2,1)S(1)}, u32[]{:S(2)}, u32[]{:S(2)}) %collective-permute-start.12) | collective-permute-done | bytes 86048 | tf_op jit(solution)/shard_map/over_chip2/ppermute | solution.py:288
  83.8 0.0 collective-permute-done.13.refs_4_
  83.8 0.6 chip_sum_kernel.1
  84.4 1.5 %collective-permute-start.15 = (bf16[96,384]{1,0:T(8,128)(2,1)S(1)}, bf16[96,384]{1,0:T(8,128)(2,1)S(1)}, u32[]{:S(2)}, u32[]{:S(2)}) collective-permute-start(bf16[96,384]{1,0:T(8,128)(2,1)S(1)} %get-tuple-element.44.refs_0_), channel_id=1, source_target_pairs={{0,8},{8,0},{16,24},{24,16},{32,40},{40,32},{48,56},{56,48},{64,72... | collective-permute-start | bytes 221192 | tf_op jit(solution)/shard_map/over_x1/ppermute | solution.py:293
  85.9 2.1 %collective-permute-start.21 = (bf16[4,48,384]{2,1,0:T(8,128)(2,1)S(1)}, bf16[4,48,384]{2,1,0:T(8,128)(2,1)S(1)}, u32[]{:S(2)}, u32[]{:S(2)}) collective-permute-start(bf16[4,48,384]{2,1,0:T(8,128)(2,1)S(1)} %get-tuple-element.45), channel_id=1, source_target_pairs={{0,4},{1,5},{2,6},{3,7},{4,0},{5,1},{6,2},{7,3},{8,12},{9,13},{10,... | collective-permute-start | bytes 442376 | tf_op jit(solution)/shard_map/forward_exit_chip2/ppermute | solution.py:288
  88.0 2.7 %collective-permute-start.16 = (bf16[96,384]{1,0:T(8,128)(2,1)S(1)}, bf16[96,384]{1,0:T(8,128)(2,1)S(1)}, u32[]{:S(2)}, u32[]{:S(2)}) collective-permute-start(bf16[96,384]{1,0:T(8,128)(2,1)S(1)} %get-tuple-element.44.refs_0_), channel_id=1, source_target_pairs={{0,16},{8,24},{16,0},{24,8},{32,48},{40,56},{48,32},{56,40},{64,80... | collective-permute-start | bytes 221192 | tf_op jit(solution)/shard_map/over_x2/ppermute | solution.py:293
  90.7 0.5 collective-permute-start.17
  91.2 0.1 collective-permute-start.23
  91.3 0.0 collective-permute-done.15.refs_1_
  91.3 2.4 %collective-permute-start.24 = (bf16[8,48,384]{2,1,0:T(8,128)(2,1)S(1)}, bf16[8,48,384]{2,1,0:T(8,128)(2,1)S(1)}, u32[]{:S(2)}, u32[]{:S(2)}) collective-permute-start(bf16[8,48,384]{2,1,0:T(8,128)(2,1)S(1)} %get-tuple-element.47), channel_id=1, source_target_pairs={{0,6},{1,7},{2,4},{3,5},{4,2},{5,3},{6,0},{7,1},{8,14},{9,15},{10,... | collective-permute-start | bytes 884744 | tf_op jit(solution)/shard_map/forward_exit_chip3/ppermute | solution.py:288
  93.7 0.2 collective-permute-done.16.refs_2_
  93.9 2.4 %collective-permute-done.17.refs_3_ = bf16[96,384]{1,0:T(8,128)(2,1)S(1)} collective-permute-done((bf16[96,384]{1,0:T(8,128)(2,1)S(1)}, bf16[96,384]{1,0:T(8,128)(2,1)S(1)}, u32[]{:S(2)}, u32[]{:S(2)}) %collective-permute-start.17) | collective-permute-done | bytes 73760 | tf_op jit(solution)/shard_map/over_x3/ppermute | solution.py:293
  96.3 1.7 %collective-permute-start.18 = (bf16[96,384]{1,0:T(8,128)(2,1)S(1)}, bf16[96,384]{1,0:T(8,128)(2,1)S(1)}, u32[]{:S(2)}, u32[]{:S(2)}) collective-permute-start(bf16[96,384]{1,0:T(8,128)(2,1)S(1)} %four_sum_kernel.2.refs_0_), channel_id=1, source_target_pairs={{0,64},{8,72},{16,80},{24,88},{32,96},{40,104},{48,112},{56,120},{... | collective-permute-start | bytes 221192 | tf_op jit(solution)/shard_map/over_y1/ppermute | solution.py:293
  98.0 2.9 %collective-permute-start.19 = (bf16[96,384]{1,0:T(8,128)(2,1)S(1)}, bf16[96,384]{1,0:T(8,128)(2,1)S(1)}, u32[]{:S(2)}, u32[]{:S(2)}) collective-permute-start(bf16[96,384]{1,0:T(8,128)(2,1)S(1)} %four_sum_kernel.2.refs_0_), channel_id=1, source_target_pairs={{0,128},{8,136},{16,144},{24,152},{32,160},{40,168},{48,176},{56,1... | collective-permute-start | bytes 221192 | tf_op jit(solution)/shard_map/over_y2/ppermute | solution.py:293
  100.9 0.0 collective-permute-done.21
  100.9 0.2 collective-permute-start.20
  101.2 0.1 collective-permute-done.18.refs_1_
  101.2 2.8 %collective-permute-done.19.refs_2_ = bf16[96,384]{1,0:T(8,128)(2,1)S(1)} collective-permute-done((bf16[96,384]{1,0:T(8,128)(2,1)S(1)}, bf16[96,384]{1,0:T(8,128)(2,1)S(1)}, u32[]{:S(2)}, u32[]{:S(2)}) %collective-permute-start.19) | collective-permute-done | bytes 73760 | tf_op jit(solution)/shard_map/over_y2/ppermute | solution.py:293
  104.0 2.4 %collective-permute-done.20.refs_3_ = bf16[96,384]{1,0:T(8,128)(2,1)S(1)} collective-permute-done((bf16[96,384]{1,0:T(8,128)(2,1)S(1)}, bf16[96,384]{1,0:T(8,128)(2,1)S(1)}, u32[]{:S(2)}, u32[]{:S(2)}) %collective-permute-start.20) | collective-permute-done | bytes 73760 | tf_op jit(solution)/shard_map/over_y3/ppermute | solution.py:293
  106.5 5.8 %collective-permute-start.22 = (bf16[96,384]{1,0:T(8,128)(2,1)S(1)}, bf16[96,384]{1,0:T(8,128)(2,1)S(1)}, u32[]{:S(2)}, u32[]{:S(2)}) collective-permute-start(bf16[96,384]{1,0:T(8,128)(2,1)S(1)} %four_sum_kernel.3.refs_1_), channel_id=1, source_target_pairs={{0,32},{8,40},{16,48},{24,56},{32,0},{40,8},{48,16},{56,24},{64,96... | collective-permute-start | bytes 221192 | tf_op jit(solution)/shard_map/over_z/ppermute | solution.py:293
  112.3 3.1 %collective-permute-done.22.refs_2_ = bf16[96,384]{1,0:T(8,128)(2,1)S(1)} collective-permute-done((bf16[96,384]{1,0:T(8,128)(2,1)S(1)}, bf16[96,384]{1,0:T(8,128)(2,1)S(1)}, u32[]{:S(2)}, u32[]{:S(2)}) %collective-permute-start.22) | collective-permute-done | bytes 73760 | tf_op jit(solution)/shard_map/over_z/ppermute | solution.py:293
  115.4 0.0 collective-permute-done.23.refs_5_
  115.4 0.0 collective-permute-done.24.refs_7_
  115.4 1.5 %final_kernel.1 = (bf16[16,2,48,384]{3,2,1,0:T(8,128)(2,1)}, f32[2,48,384]{2,1,0:T(8,128)}) custom-call(s32[1]{0:T(128)} %bitcast.refs_0_, bf16[96,384]{1,0:T(8,128)(2,1)S(1)} %four_sum_kernel.3.refs_1_, bf16[96,384]{1,0:T(8,128)(2,1)S(1)} %collective-permute-done.22.refs_2_, bf16[4,4,48,384]{3,2,1,0:T(8,128)(2,1)S(1)} %get-tuple-element.43.refs_3_, ...), custom_call_target="tpu_custom_call" | custom-call | bytes 3538948 | tf_op jit(solution)/shard_map/final_kernel/pallas_call | solution.py:271
  (26 shorter events, 0.6 us)
Async XLA Ops:
  0.6 1.3 %copy-start.1 = (bf16[16,2,48,384]{3,2,1,0:T(8,128)(2,1)S(1)}, bf16[16,2,48,384]{3,2,1,0:T(8,128)(2,1)}, u32[]{:S(2)}) copy-start(bf16[16,2,48,384]{3,2,1,0:T(8,128)(2,1)} %param.5) | copy-start | bytes 3538948
  1.9 1.3 %copy-start.3 = (bf16[16,2,48,384]{3,2,1,0:T(8,128)(2,1)S(1)}, bf16[16,2,48,384]{3,2,1,0:T(8,128)(2,1)}, u32[]{:S(2)}) copy-start(bf16[16,2,48,384]{3,2,1,0:T(8,128)(2,1)} %refs_1_.2) | copy-start | bytes 3538948
  2.0 3.3 %copy-start.4 = (f32[48,384]{1,0:T(8,128)S(1)}, f32[48,384]{1,0:T(8,128)}, u32[]{:S(2)}) copy-start(f32[48,384]{1,0:T(8,128)} %param.9) | copy-start | bytes 221188
  2.0 3.4 %collective-permute-start = (bf16[4,4,48,384]{3,2,1,0:T(8,128)(2,1)S(1)}, bf16[4,4,48,384]{3,2,1,0:T(8,128)(2,1)S(1)}, u32[]{:S(2)}, u32[]{:S(2)}) collective-permute-start(bf16[4,4,48,384]{3,2,1,0:T(8,128)(2,1)S(1)} %get-tuple-element.29), channel_id=1, source_target_pairs={{0,1},{1,0},{2,3},{3,2},{4,5},{5,4},{6,7},{7,6},{8,9},{9,8},{10,11... | collective-permute-start | bytes 1769480 | tf_op jit(solution)/shard_map/forward_entry_core/ppermute | solution.py:288
  5.2 5.1 %collective-permute-start.3 = (bf16[4,4,48,384]{3,2,1,0:T(8,128)(2,1)S(1)}, bf16[4,4,48,384]{3,2,1,0:T(8,128)(2,1)S(1)}, u32[]{:S(2)}, u32[]{:S(2)}) collective-permute-start(bf16[4,4,48,384]{3,2,1,0:T(8,128)(2,1)S(1)} %get-tuple-element.30), channel_id=1, source_target_pairs={{0,1},{1,0},{2,3},{3,2},{4,5},{5,4},{6,7},{7,6},{8,9},{9,8},{10,11... | collective-permute-start | bytes 1769480 | tf_op jit(solution)/shard_map/backward_entry_core/ppermute | solution.py:288
  5.5 17.3 %copy-start = (f32[3,384,384]{2,1,0:T(8,128)S(1)}, f32[3,384,384]{2,1,0:T(8,128)}, u32[]{:S(2)}) copy-start(f32[3,384,384]{2,1,0:T(8,128)} %refs_2_.1) | copy-start | bytes 5308420
  5.5 17.3 %copy-start.2 = (s32[16]{0:T(128)S(1)}, s32[16]{0:T(128)}, u32[]{:S(2)}) copy-start(s32[16]{0:T(128)} %refs_1_.3) | copy-start | bytes 196
  5.6 17.1 %collective-permute-start.2 = (bf16[9,48,384]{2,1,0:T(8,128)(2,1)S(1)}, bf16[9,48,384]{2,1,0:T(8,128)(2,1)S(1)}, u32[]{:S(2)}, u32[]{:S(2)}) collective-permute-start(bf16[9,48,384]{2,1,0:T(8,128)(2,1)S(1)} %get-tuple-element.70), channel_id=1, source_target_pairs={{0,2},{1,3},{2,0},{3,1},{4,6},{5,7},{6,4},{7,5},{8,10},{9,11},{10,... | collective-permute-start | bytes 995336 | tf_op jit(solution)/shard_map/forward_entry_chip1/ppermute | solution.py:288
  5.9 26.1 %collective-permute-start.1 = (bf16[9,48,384]{2,1,0:T(8,128)(2,1)S(1)}, bf16[9,48,384]{2,1,0:T(8,128)(2,1)S(1)}, u32[]{:S(2)}, u32[]{:S(2)}) collective-permute-start(bf16[9,48,384]{2,1,0:T(8,128)(2,1)S(1)} %get-tuple-element.71), channel_id=1, source_target_pairs={{0,4},{1,5},{2,6},{3,7},{4,0},{5,1},{6,2},{7,3},{8,12},{9,13},{10,... | collective-permute-start | bytes 995336 | tf_op jit(solution)/shard_map/forward_entry_chip2/ppermute | solution.py:288
  9.2 27.6 %collective-permute-start.7 = (bf16[9,48,384]{2,1,0:T(8,128)(2,1)S(1)}, bf16[9,48,384]{2,1,0:T(8,128)(2,1)S(1)}, u32[]{:S(2)}, u32[]{:S(2)}) collective-permute-start(bf16[9,48,384]{2,1,0:T(8,128)(2,1)S(1)} %get-tuple-element.69), channel_id=1, source_target_pairs={{0,6},{1,7},{2,4},{3,5},{4,2},{5,3},{6,0},{7,1},{8,14},{9,15},{10,... | collective-permute-start | bytes 995336 | tf_op jit(solution)/shard_map/forward_entry_chip3/ppermute | solution.py:288
  32.1 10.8 %collective-permute-start.4 = (bf16[8,48,384]{2,1,0:T(8,128)(2,1)S(1)}, bf16[8,48,384]{2,1,0:T(8,128)(2,1)S(1)}, u32[]{:S(2)}, u32[]{:S(2)}) collective-permute-start(bf16[8,48,384]{2,1,0:T(8,128)(2,1)S(1)} %pad_maximum_fusion.3), channel_id=1, source_target_pairs={{0,2},{1,3},{2,0},{3,1},{4,6},{5,7},{6,4},{7,5},{8,10},{9,11},{10,... | collective-permute-start | bytes 884744 | tf_op jit(solution)/shard_map/backward_entry_chip1/ppermute | solution.py:288
  32.3 25.8 %collective-permute-start.5 = (bf16[8,48,384]{2,1,0:T(8,128)(2,1)S(1)}, bf16[8,48,384]{2,1,0:T(8,128)(2,1)S(1)}, u32[]{:S(2)}, u32[]{:S(2)}) collective-permute-start(bf16[8,48,384]{2,1,0:T(8,128)(2,1)S(1)} %pad_maximum_fusion.4), channel_id=1, source_target_pairs={{0,4},{1,5},{2,6},{3,7},{4,0},{5,1},{6,2},{7,3},{8,12},{9,13},{10,... | collective-permute-start | bytes 884744 | tf_op jit(solution)/shard_map/backward_entry_chip2/ppermute | solution.py:288
  35.4 22.7 %collective-permute-start.6 = (bf16[8,48,384]{2,1,0:T(8,128)(2,1)S(1)}, bf16[8,48,384]{2,1,0:T(8,128)(2,1)S(1)}, u32[]{:S(2)}, u32[]{:S(2)}) collective-permute-start(bf16[8,48,384]{2,1,0:T(8,128)(2,1)S(1)} %pad_maximum_fusion.5), channel_id=1, source_target_pairs={{0,6},{1,7},{2,4},{3,5},{4,2},{5,3},{6,0},{7,1},{8,14},{9,15},{10,... | collective-permute-start | bytes 884744 | tf_op jit(solution)/shard_map/backward_entry_chip3/ppermute | solution.py:288
  36.9 5.4 %collective-permute-start.8 = (bf16[4,48,384]{2,1,0:T(8,128)(2,1)S(1)}, bf16[4,48,384]{2,1,0:T(8,128)(2,1)S(1)}, u32[]{:S(2)}, u32[]{:S(2)}) collective-permute-start(bf16[4,48,384]{2,1,0:T(8,128)(2,1)S(1)} %pad_maximum_fusion.8.refs_1_), channel_id=1, source_target_pairs={{0,1},{1,0},{2,3},{3,2},{4,5},{5,4},{6,7},{7,6},{8,9},{9,8},{10,11... | collective-permute-start | bytes 442376 | tf_op jit(solution)/shard_map/mask_core/ppermute | solution.py:288
  41.8 28.7 %collective-permute-start.10 = (bf16[4,4,48,384]{3,2,1,0:T(8,128)(2,1)S(1)}, bf16[4,4,48,384]{3,2,1,0:T(8,128)(2,1)S(1)}, u32[]{:S(2)}, u32[]{:S(2)}) collective-permute-start(bf16[4,4,48,384]{3,2,1,0:T(8,128)(2,1)S(1)} %get-tuple-element.38), channel_id=1, source_target_pairs={{0,1},{1,0},{2,3},{3,2},{4,5},{5,4},{6,7},{7,6},{8,9},{9,8},{10,11... | collective-permute-start | bytes 1769480 | tf_op jit(solution)/shard_map/forward_exit_core/ppermute | solution.py:288
  62.7 7.8 %collective-permute-start.9 = (bf16[400,384]{1,0:T(8,128)(2,1)S(1)}, bf16[400,384]{1,0:T(8,128)(2,1)S(1)}, u32[]{:S(2)}, u32[]{:S(2)}) collective-permute-start(bf16[400,384]{1,0:T(8,128)(2,1)S(1)} %get-tuple-element.37), channel_id=1, source_target_pairs={{0,1},{1,0},{2,3},{3,2},{4,5},{5,4},{6,7},{7,6},{8,9},{9,8},{10,11... | collective-permute-start | bytes 921608 | tf_op jit(solution)/shard_map/over_core/ppermute | solution.py:288
  62.9 19.1 %collective-permute-start.14 = (bf16[4,48,384]{2,1,0:T(8,128)(2,1)S(1)}, bf16[4,48,384]{2,1,0:T(8,128)(2,1)S(1)}, u32[]{:S(2)}, u32[]{:S(2)}) collective-permute-start(bf16[4,48,384]{2,1,0:T(8,128)(2,1)S(1)} %get-tuple-element.53), channel_id=1, source_target_pairs={{0,4},{1,5},{2,6},{3,7},{4,0},{5,1},{6,2},{7,3},{8,12},{9,13},{10,... | collective-permute-start | bytes 442376 | tf_op jit(solution)/shard_map/forward_exit_start2/ppermute | solution.py:288
  70.6 11.4 %collective-permute-start.11 = (bf16[112,384]{1,0:T(8,128)(2,1)S(1)}, bf16[112,384]{1,0:T(8,128)(2,1)S(1)}, u32[]{:S(2)}, u32[]{:S(2)}) collective-permute-start(bf16[112,384]{1,0:T(8,128)(2,1)S(1)} %get-tuple-element.40), channel_id=1, source_target_pairs={{0,2},{1,3},{2,0},{3,1},{4,6},{5,7},{6,4},{7,5},{8,10},{9,11},{10,... | collective-permute-start | bytes 258056 | tf_op jit(solution)/shard_map/over_chip1/ppermute | solution.py:288
  71.0 12.8 %collective-permute-start.12 = (bf16[112,384]{1,0:T(8,128)(2,1)S(1)}, bf16[112,384]{1,0:T(8,128)(2,1)S(1)}, u32[]{:S(2)}, u32[]{:S(2)}) collective-permute-start(bf16[112,384]{1,0:T(8,128)(2,1)S(1)} %get-tuple-element.41), channel_id=1, source_target_pairs={{0,4},{1,5},{2,6},{3,7},{4,0},{5,1},{6,2},{7,3},{8,12},{9,13},{10,... | collective-permute-start | bytes 258056 | tf_op jit(solution)/shard_map/over_chip2/ppermute | solution.py:288
  72.6 11.2 %collective-permute-start.13 = (bf16[112,384]{1,0:T(8,128)(2,1)S(1)}, bf16[112,384]{1,0:T(8,128)(2,1)S(1)}, u32[]{:S(2)}, u32[]{:S(2)}) collective-permute-start(bf16[112,384]{1,0:T(8,128)(2,1)S(1)} %get-tuple-element.42), channel_id=1, source_target_pairs={{0,6},{1,7},{2,4},{3,5},{4,2},{5,3},{6,0},{7,1},{8,14},{9,15},{10,... | collective-permute-start | bytes 258056 | tf_op jit(solution)/shard_map/over_chip3/ppermute | solution.py:288
  84.4 6.9 %collective-permute-start.15 = (bf16[96,384]{1,0:T(8,128)(2,1)S(1)}, bf16[96,384]{1,0:T(8,128)(2,1)S(1)}, u32[]{:S(2)}, u32[]{:S(2)}) collective-permute-start(bf16[96,384]{1,0:T(8,128)(2,1)S(1)} %get-tuple-element.44.refs_0_), channel_id=1, source_target_pairs={{0,8},{8,0},{16,24},{24,16},{32,40},{40,32},{48,56},{56,48},{64,72... | collective-permute-start | bytes 221192 | tf_op jit(solution)/shard_map/over_x1/ppermute | solution.py:293
  85.9 15.0 %collective-permute-start.21 = (bf16[4,48,384]{2,1,0:T(8,128)(2,1)S(1)}, bf16[4,48,384]{2,1,0:T(8,128)(2,1)S(1)}, u32[]{:S(2)}, u32[]{:S(2)}) collective-permute-start(bf16[4,48,384]{2,1,0:T(8,128)(2,1)S(1)} %get-tuple-element.45), channel_id=1, source_target_pairs={{0,4},{1,5},{2,6},{3,7},{4,0},{5,1},{6,2},{7,3},{8,12},{9,13},{10,... | collective-permute-start | bytes 442376 | tf_op jit(solution)/shard_map/forward_exit_chip2/ppermute | solution.py:288
  88.0 5.9 %collective-permute-start.16 = (bf16[96,384]{1,0:T(8,128)(2,1)S(1)}, bf16[96,384]{1,0:T(8,128)(2,1)S(1)}, u32[]{:S(2)}, u32[]{:S(2)}) collective-permute-start(bf16[96,384]{1,0:T(8,128)(2,1)S(1)} %get-tuple-element.44.refs_0_), channel_id=1, source_target_pairs={{0,16},{8,24},{16,0},{24,8},{32,48},{40,56},{48,32},{56,40},{64,80... | collective-permute-start | bytes 221192 | tf_op jit(solution)/shard_map/over_x2/ppermute | solution.py:293
  90.7 5.6 %collective-permute-start.17 = (bf16[96,384]{1,0:T(8,128)(2,1)S(1)}, bf16[96,384]{1,0:T(8,128)(2,1)S(1)}, u32[]{:S(2)}, u32[]{:S(2)}) collective-permute-start(bf16[96,384]{1,0:T(8,128)(2,1)S(1)} %get-tuple-element.44.refs_0_), channel_id=1, source_target_pairs={{0,24},{8,16},{16,8},{24,0},{32,56},{40,48},{48,40},{56,32},{64,88... | collective-permute-start | bytes 221192 | tf_op jit(solution)/shard_map/over_x3/ppermute | solution.py:293
  91.2 24.2 %collective-permute-start.23 = (bf16[8,48,384]{2,1,0:T(8,128)(2,1)S(1)}, bf16[8,48,384]{2,1,0:T(8,128)(2,1)S(1)}, u32[]{:S(2)}, u32[]{:S(2)}) collective-permute-start(bf16[8,48,384]{2,1,0:T(8,128)(2,1)S(1)} %get-tuple-element.46), channel_id=1, source_target_pairs={{0,2},{1,3},{2,0},{3,1},{4,6},{5,7},{6,4},{7,5},{8,10},{9,11},{10,... | collective-permute-start | bytes 884744 | tf_op jit(solution)/shard_map/forward_exit_chip1/ppermute | solution.py:288
  91.3 24.1 %collective-permute-start.24 = (bf16[8,48,384]{2,1,0:T(8,128)(2,1)S(1)}, bf16[8,48,384]{2,1,0:T(8,128)(2,1)S(1)}, u32[]{:S(2)}, u32[]{:S(2)}) collective-permute-start(bf16[8,48,384]{2,1,0:T(8,128)(2,1)S(1)} %get-tuple-element.47), channel_id=1, source_target_pairs={{0,6},{1,7},{2,4},{3,5},{4,2},{5,3},{6,0},{7,1},{8,14},{9,15},{10,... | collective-permute-start | bytes 884744 | tf_op jit(solution)/shard_map/forward_exit_chip3/ppermute | solution.py:288
  96.3 4.9 %collective-permute-start.18 = (bf16[96,384]{1,0:T(8,128)(2,1)S(1)}, bf16[96,384]{1,0:T(8,128)(2,1)S(1)}, u32[]{:S(2)}, u32[]{:S(2)}) collective-permute-start(bf16[96,384]{1,0:T(8,128)(2,1)S(1)} %four_sum_kernel.2.refs_0_), channel_id=1, source_target_pairs={{0,64},{8,72},{16,80},{24,88},{32,96},{40,104},{48,112},{56,120},{... | collective-permute-start | bytes 221192 | tf_op jit(solution)/shard_map/over_y1/ppermute | solution.py:293
  98.0 6.0 %collective-permute-start.19 = (bf16[96,384]{1,0:T(8,128)(2,1)S(1)}, bf16[96,384]{1,0:T(8,128)(2,1)S(1)}, u32[]{:S(2)}, u32[]{:S(2)}) collective-permute-start(bf16[96,384]{1,0:T(8,128)(2,1)S(1)} %four_sum_kernel.2.refs_0_), channel_id=1, source_target_pairs={{0,128},{8,136},{16,144},{24,152},{32,160},{40,168},{48,176},{56,1... | collective-permute-start | bytes 221192 | tf_op jit(solution)/shard_map/over_y2/ppermute | solution.py:293
  100.9 5.6 %collective-permute-start.20 = (bf16[96,384]{1,0:T(8,128)(2,1)S(1)}, bf16[96,384]{1,0:T(8,128)(2,1)S(1)}, u32[]{:S(2)}, u32[]{:S(2)}) collective-permute-start(bf16[96,384]{1,0:T(8,128)(2,1)S(1)} %four_sum_kernel.2.refs_0_), channel_id=1, source_target_pairs={{0,192},{8,200},{16,208},{24,216},{32,224},{40,232},{48,240},{56,2... | collective-permute-start | bytes 221192 | tf_op jit(solution)/shard_map/over_y3/ppermute | solution.py:293
  106.5 8.9 %collective-permute-start.22 = (bf16[96,384]{1,0:T(8,128)(2,1)S(1)}, bf16[96,384]{1,0:T(8,128)(2,1)S(1)}, u32[]{:S(2)}, u32[]{:S(2)}) collective-permute-start(bf16[96,384]{1,0:T(8,128)(2,1)S(1)} %four_sum_kernel.3.refs_1_), channel_id=1, source_target_pairs={{0,32},{8,40},{16,48},{24,56},{32,0},{40,8},{48,16},{56,24},{64,96... | collective-permute-start | bytes 221192 | tf_op jit(solution)/shard_map/over_z/ppermute | solution.py:293

commit v2 on v1

--- a/solution.py
+++ b/solution.py
@@ -211,9 +211,12 @@
     return (terms[0] + terms[1]) + (terms[2] + terms[3])
 
 
-def chip_sum_kernel(at_ref, *refs):
-    parts, (over_ref, coup_ref) = refs[:CHIPS], refs[-2:]
-    over_ref[...] = four([p[: 2 * PIECE, :] for p in parts]).astype(BF16)
+def chip_sum_kernel(*refs):
+    refs[-1][...] = four([p[: 2 * PIECE, :] for p in refs[:CHIPS]]).astype(BF16)
+
+
+def coupling_kernel(at_ref, *refs):
+    parts, coup_ref = refs[:CHIPS], refs[-1]
     at = lax.broadcasted_iota(jnp.int32, (1, 128), 1)
     result = [jnp.zeros((1, 128), F32)] * 2
     for k in range(ROWS):
@@ -360,14 +363,8 @@
     )
     parts = [sums[0]] + [over_rows(sums[j], 2 * j, f"over_chip{j}") for j in range(1, CHIPS)]
     small = ((2 * PIECE, N), BF16)
-    over, coupling, *pairs = call(
-        chip_sum_kernel,
-        [at, *parts],
-        [small, ((2, ROWS * MINE), F32)],
-        after=[start1],
-        through=pairs,
-
-    )
+    over, *pairs = call(chip_sum_kernel, parts, [small], after=[start1], through=pairs)
+    (coupling,) = call(coupling_kernel, [at, *parts], [((2, ROWS * MINE), F32)])
     near, far, last = [
         over_rows(p, 2 * j + 2, f"forward_exit_chip{j + 1}") for j, p in enumerate(pairs)
     ]
@@ -375,7 +372,7 @@
     terms = [over] + [over_modes(over, k, f"over_x{k}") for k in X_STEPS]
     (over,) = call(four_sum_kernel, terms, [small])
     terms = [over] + [over_modes(over, k, f"over_y{k // 8}") for k in Y_STEPS]
-    (over,) = call(four_sum_kernel, terms, [small], after=[far])
+    (over,) = call(four_sum_kernel, terms, [small], after=[far, coupling])
     fwd_out, new_mask = call(
         final_kernel,
         [at, over, over_modes(over, Z_STEP, "over_z"), keep, got, near, far, last],

time: 117 us -> 118 us (level)
    unnamed x11 -> x13, local copies, waits for them, and re-layouts: 2.35 us -> 3.03 us
    pallas_call x12 -> x13, Pallas kernels: 15.9 us -> 15.9 us  [call(): pl.pallas_call(body, name=kernel.__name__, out_shape=[jax.ShapeDtypeStruc...]
  transfers between devices with their start and end apart: 25 -> 25, of which waited for: 11 -> 10; matrix products, arithmetic and copies ran while one was open for 1% -> 1% of each run, Pallas kernels for 12% -> 12%
where the time goes in v2:
time: 118 us; the launch traced here: 117 us
  waiting for transfers between devices  54.3 us (46%)
  starting transfers between devices  42.5 us (36%)
  Pallas kernels  15.9 us (13%)
  local copies, waits for them, and re-layouts  3.34 us (3%)
    ppermute x18, waiting for transfers between devices, over_rows(): return lax.ppermute(block, 'rows', [(s, s ^ k) for s in range(ROWS)])  43.9 us
    ppermute x18, starting transfers between devices, over_rows(): return lax.ppermute(block, 'rows', [(s, s ^ k) for s in range(ROWS)])  26.9 us
    pallas_call x13, Pallas kernels, call(): pl.pallas_call(body, name=kernel.__name__, out_shape=[jax.ShapeDtypeStruc...  15.9 us
    ppermute x7, starting transfers between devices, over_modes(): lax.ppermute(block, 'modes', [(s, s ^ k) for s in range(lax.axis_size('mo...  15.6 us
    ppermute x7, waiting for transfers between devices, over_modes(): lax.ppermute(block, 'modes', [(s, s ^ k) for s in range(lax.axis_size('mo...  10.4 us
    unnamed x13, local copies, waits for them, and re-layouts  3.03 us
  transfers between devices with their start and end apart: 25, of which 10 were waited for; matrix products, arithmetic and copies ran while one was open for 1% of the time, Pallas kernels for 12%

profile of v2, /device:TPU:0, one launch (start us, length us, event | category | flops | bytes accessed | tf_op | source)
XLA Modules:
  0.0 117.4 jit_solution(11998612321896348671)
XLA Ops:
  0.6 1.3 %copy-done.1 = bf16[16,2,48,384]{3,2,1,0:T(8,128)(2,1)S(1)} copy-done((bf16[16,2,48,384]{3,2,1,0:T(8,128)(2,1)S(1)}, bf16[16,2,48,384]{3,2,1,0:T(8,128)(2,1)}, u32[]{:S(2)}) %copy-start.1) | copy-done | bytes 1179672
  1.9 0.1 cut_kernel.1
  2.0 0.0 copy-start.5
  2.0 0.1 collective-permute-start
  2.1 1.1 copy-done.4
  3.2 2.0 %tables_kernel.1 = (bf16[768,768]{1,0:T(8,128)(2,1)S(1)}, bf16[768,768]{1,0:T(8,128)(2,1)S(1)}, bf16[4,4,48,384]{3,2,1,0:T(8,128)(2,1)S(1)}, bf16[4,4,48,384]{3,2,1,0:T(8,128)(2,1)S(1)}) custom-call(s32[1]{0:T(128)} %bitcast.refs_0_, bf16[16,2,48,384]{3,2,1,0:T(8,128)(2,1)S(1)} %copy-done.4), custom_call_target="tpu_custom_call" | custom-call | flops 905969664 | bytes 4718596 | tf_op jit(solution)/shard_map/tables_kernel/pallas_call | solution.py:274
  5.2 0.1 collective-permute-start.3
  5.4 0.0 collective-permute-done.refs_2_
  5.5 0.0 copy-start
  5.5 0.0 copy-start.3
  5.5 0.2 pad_maximum_fusion
  5.6 0.3 collective-permute-start.2
  5.9 3.3 %collective-permute-start.1 = (bf16[9,48,384]{2,1,0:T(8,128)(2,1)S(1)}, bf16[9,48,384]{2,1,0:T(8,128)(2,1)S(1)}, u32[]{:S(2)}, u32[]{:S(2)}) collective-permute-start(bf16[9,48,384]{2,1,0:T(8,128)(2,1)S(1)} %get-tuple-element.69), channel_id=1, source_target_pairs={{0,4},{1,5},{2,6},{3,7},{4,0},{5,1},{6,2},{7,3},{8,12},{9,13},{10,... | collective-permute-start | bytes 995336 | tf_op jit(solution)/shard_map/forward_entry_chip2/ppermute | solution.py:291
  9.2 1.0 collective-permute-start.7
  10.3 0.0 collective-permute-done.3.refs_4_
  10.3 12.5 %collective-permute-done.2.refs_3_ = bf16[9,48,384]{2,1,0:T(8,128)(2,1)S(1)} collective-permute-done((bf16[9,48,384]{2,1,0:T(8,128)(2,1)S(1)}, bf16[9,48,384]{2,1,0:T(8,128)(2,1)S(1)}, u32[]{:S(2)}, u32[]{:S(2)}) %collective-permute-start.2) | collective-permute-done | bytes 331808 | tf_op jit(solution)/shard_map/forward_entry_chip1/ppermute | solution.py:291
  22.7 1.7 %trig_kernel.1 = (f32[2,2,384,384]{3,2,1,0:T(8,128)S(1)}, bf16[4,4,48,384]{3,2,1,0:T(8,128)(2,1)S(1)}) custom-call(s32[1]{0:T(128)} %bitcast.refs_0_, s32[16]{0:T(128)S(1)} %copy-done.3, f32[3,384,384]{2,1,0:T(8,128)S(1)} %copy-done, bf16[9,48,384]{2,1,0:T(8,128)(2,1)S(1)} %collective-permute-done.2.refs_3_, ...), custom_call_target="tpu_custom_call", output_to_operand_aliasing={{1}: (4, {})} | custom-call | bytes 4128836 | tf_op jit(solution)/shard_map/trig_kernel/pallas_call | solution.py:274
  24.5 7.6 %collective-permute-done.1.refs_1_.refs_4_ = bf16[9,48,384]{2,1,0:T(8,128)(2,1)S(1)} collective-permute-done((bf16[9,48,384]{2,1,0:T(8,128)(2,1)S(1)}, bf16[9,48,384]{2,1,0:T(8,128)(2,1)S(1)}, u32[]{:S(2)}, u32[]{:S(2)}) %collective-permute-start.1) | collective-permute-done | bytes 331808 | tf_op jit(solution)/shard_map/forward_entry_chip2/ppermute | solution.py:291
  32.1 0.1 collective-permute-start.4
  32.3 3.1 %collective-permute-start.5 = (bf16[8,48,384]{2,1,0:T(8,128)(2,1)S(1)}, bf16[8,48,384]{2,1,0:T(8,128)(2,1)S(1)}, u32[]{:S(2)}, u32[]{:S(2)}) collective-permute-start(bf16[8,48,384]{2,1,0:T(8,128)(2,1)S(1)} %pad_maximum_fusion.4), channel_id=1, source_target_pairs={{0,4},{1,5},{2,6},{3,7},{4,0},{5,1},{6,2},{7,3},{8,12},{9,13},{10,... | collective-permute-start | bytes 884744 | tf_op jit(solution)/shard_map/backward_entry_chip2/ppermute | solution.py:291
  35.4 1.4 %collective-permute-start.6 = (bf16[8,48,384]{2,1,0:T(8,128)(2,1)S(1)}, bf16[8,48,384]{2,1,0:T(8,128)(2,1)S(1)}, u32[]{:S(2)}, u32[]{:S(2)}) collective-permute-start(bf16[8,48,384]{2,1,0:T(8,128)(2,1)S(1)} %pad_maximum_fusion.5), channel_id=1, source_target_pairs={{0,6},{1,7},{2,4},{3,5},{4,2},{5,3},{6,0},{7,1},{8,14},{9,15},{10,... | collective-permute-start | bytes 884744 | tf_op jit(solution)/shard_map/backward_entry_chip3/ppermute | solution.py:291
  36.9 0.0 collective-permute-done.7.refs_5_
  36.9 0.3 collective-permute-start.8
  37.2 4.5 %forward_kernel.1 = (f32[2,384,768]{2,1,0:T(8,128)S(1)}, bf16[4,4,48,384]{3,2,1,0:T(8,128)(2,1)S(1)}, bf16[4,4,48,384]{3,2,1,0:T(8,128)(2,1)S(1)}) custom-call(s32[1]{0:T(128)} %bitcast.refs_0_, bf16[4,4,48,384]{3,2,1,0:T(8,128)(2,1)S(1)} %get-tuple-element.27.refs_1_, bf16[4,4,48,384]{3,2,1,0:T(8,128)(2,1)S(1)} %collective-permute-done.refs_2_, ...), custom_call_target="tpu_custom_call" | custom-call | flops 3623878656 | bytes 10432516 | tf_op jit(solution)/shard_map/forward_kernel/pallas_call | solution.py:274
  41.8 0.6 collective-permute-start.10
  42.3 0.0 collective-permute-done.8.refs_2_
  42.3 0.6 mask_kernel.1.refs_10_
  42.9 0.0 collective-permute-done.4.refs_3_
  42.9 15.2 %collective-permute-done.5.refs_4_ = bf16[8,48,384]{2,1,0:T(8,128)(2,1)S(1)} collective-permute-done((bf16[8,48,384]{2,1,0:T(8,128)(2,1)S(1)}, bf16[8,48,384]{2,1,0:T(8,128)(2,1)S(1)}, u32[]{:S(2)}, u32[]{:S(2)}) %collective-permute-start.5) | collective-permute-done | bytes 294944 | tf_op jit(solution)/shard_map/backward_entry_chip2/ppermute | solution.py:291
  58.1 0.0 collective-permute-done.6.refs_5_
  58.1 4.6 %backward_kernel.1 = (bf16[400,384]{1,0:T(8,128)(2,1)S(1)}, bf16[400,384]{1,0:T(8,128)(2,1)S(1)}) custom-call(s32[1]{0:T(128)} %bitcast.refs_0_, bf16[4,4,48,384]{3,2,1,0:T(8,128)(2,1)S(1)} %get-tuple-element.26.refs_1_, bf16[4,4,48,384]{3,2,1,0:T(8,128)(2,1)S(1)} %gate_kernel.1.refs_2_, bf16[8,48,384]{2,1,0:T(8,128)(2,1)S(1)} %collective-permute-done.4.refs_3_, ...), custom_call_target="tpu_custom_call" | custom-call | flops 2717908992 | bytes 10936324 | tf_op jit(solution)/shard_map/backward_kernel/pallas_call | solution.py:274
  62.7 0.1 collective-permute-start.9
  62.9 7.6 %collective-permute-start.14 = (bf16[4,48,384]{2,1,0:T(8,128)(2,1)S(1)}, bf16[4,48,384]{2,1,0:T(8,128)(2,1)S(1)}, u32[]{:S(2)}, u32[]{:S(2)}) collective-permute-start(bf16[4,48,384]{2,1,0:T(8,128)(2,1)S(1)} %get-tuple-element.51), channel_id=1, source_target_pairs={{0,4},{1,5},{2,6},{3,7},{4,0},{5,1},{6,2},{7,3},{8,12},{9,13},{10,... | collective-permute-start | bytes 442376 | tf_op jit(solution)/shard_map/forward_exit_start2/ppermute | solution.py:291
  70.4 0.0 collective-permute-done.10.refs_2_.refs_4_
  70.5 0.0 collective-permute-done.9.refs_1_
  70.5 0.1 core_sum_kernel.1
  70.6 0.5 collective-permute-start.11
  71.0 1.5 %collective-permute-start.12 = (bf16[112,384]{1,0:T(8,128)(2,1)S(1)}, bf16[112,384]{1,0:T(8,128)(2,1)S(1)}, u32[]{:S(2)}, u32[]{:S(2)}) collective-permute-start(bf16[112,384]{1,0:T(8,128)(2,1)S(1)} %get-tuple-element.40), channel_id=1, source_target_pairs={{0,4},{1,5},{2,6},{3,7},{4,0},{5,1},{6,2},{7,3},{8,12},{9,13},{10,... | collective-permute-start | bytes 258056 | tf_op jit(solution)/shard_map/over_chip2/ppermute | solution.py:291
  72.6 2.5 %collective-permute-start.13 = (bf16[112,384]{1,0:T(8,128)(2,1)S(1)}, bf16[112,384]{1,0:T(8,128)(2,1)S(1)}, u32[]{:S(2)}, u32[]{:S(2)}) collective-permute-start(bf16[112,384]{1,0:T(8,128)(2,1)S(1)} %get-tuple-element.41), channel_id=1, source_target_pairs={{0,6},{1,7},{2,4},{3,5},{4,2},{5,3},{6,0},{7,1},{8,14},{9,15},{10,... | collective-permute-start | bytes 258056 | tf_op jit(solution)/shard_map/over_chip3/ppermute | solution.py:291
  75.0 0.1 pad_maximum_fusion.6
  75.1 6.8 %collective-permute-done.14.refs_4_ = bf16[4,48,384]{2,1,0:T(8,128)(2,1)S(1)} collective-permute-done((bf16[4,48,384]{2,1,0:T(8,128)(2,1)S(1)}, bf16[4,48,384]{2,1,0:T(8,128)(2,1)S(1)}, u32[]{:S(2)}, u32[]{:S(2)}) %collective-permute-start.14) | collective-permute-done | bytes 147488 | tf_op jit(solution)/shard_map/forward_exit_start2/ppermute | solution.py:291
  82.0 0.0 collective-permute-done.11.refs_1_.refs_2_
  82.0 1.8 %collective-permute-done.12.refs_2_.refs_3_ = bf16[112,384]{1,0:T(8,128)(2,1)S(1)} collective-permute-done((bf16[112,384]{1,0:T(8,128)(2,1)S(1)}, bf16[112,384]{1,0:T(8,128)(2,1)S(1)}, u32[]{:S(2)}, u32[]{:S(2)}) %collective-permute-start.12) | collective-permute-done | bytes 86048 | tf_op jit(solution)/shard_map/over_chip2/ppermute | solution.py:291
  83.8 0.0 collective-permute-done.13.refs_3_.refs_4_
  83.9 1.8 %collective-permute-start.15 = (bf16[96,384]{1,0:T(8,128)(2,1)S(1)}, bf16[96,384]{1,0:T(8,128)(2,1)S(1)}, u32[]{:S(2)}, u32[]{:S(2)}) collective-permute-start(bf16[96,384]{1,0:T(8,128)(2,1)S(1)} %get-tuple-element.43.refs_0_), channel_id=1, source_target_pairs={{0,8},{8,0},{16,24},{24,16},{32,40},{40,32},{48,56},{56,48},{64,72... | collective-permute-start | bytes 221192 | tf_op jit(solution)/shard_map/over_x1/ppermute | solution.py:296
  85.7 2.1 %collective-permute-start.21 = (bf16[4,48,384]{2,1,0:T(8,128)(2,1)S(1)}, bf16[4,48,384]{2,1,0:T(8,128)(2,1)S(1)}, u32[]{:S(2)}, u32[]{:S(2)}) collective-permute-start(bf16[4,48,384]{2,1,0:T(8,128)(2,1)S(1)} %get-tuple-element.44), channel_id=1, source_target_pairs={{0,4},{1,5},{2,6},{3,7},{4,0},{5,1},{6,2},{7,3},{8,12},{9,13},{10,... | collective-permute-start | bytes 442376 | tf_op jit(solution)/shard_map/forward_exit_chip2/ppermute | solution.py:291
  87.8 2.7 %collective-permute-start.16 = (bf16[96,384]{1,0:T(8,128)(2,1)S(1)}, bf16[96,384]{1,0:T(8,128)(2,1)S(1)}, u32[]{:S(2)}, u32[]{:S(2)}) collective-permute-start(bf16[96,384]{1,0:T(8,128)(2,1)S(1)} %get-tuple-element.43.refs_0_), channel_id=1, source_target_pairs={{0,16},{8,24},{16,0},{24,8},{32,48},{40,56},{48,32},{56,40},{64,80... | collective-permute-start | bytes 221192 | tf_op jit(solution)/shard_map/over_x2/ppermute | solution.py:296
  90.5 0.5 collective-permute-start.17
  91.0 0.1 collective-permute-start.23
  91.1 2.4 %collective-permute-start.24 = (bf16[8,48,384]{2,1,0:T(8,128)(2,1)S(1)}, bf16[8,48,384]{2,1,0:T(8,128)(2,1)S(1)}, u32[]{:S(2)}, u32[]{:S(2)}) collective-permute-start(bf16[8,48,384]{2,1,0:T(8,128)(2,1)S(1)} %get-tuple-element.46), channel_id=1, source_target_pairs={{0,6},{1,7},{2,4},{3,5},{4,2},{5,3},{6,0},{7,1},{8,14},{9,15},{10,... | collective-permute-start | bytes 884744 | tf_op jit(solution)/shard_map/forward_exit_chip3/ppermute | solution.py:291
  93.5 0.6 coupling_kernel.1.refs_5_
  94.1 0.0 collective-permute-done.16.refs_2_
  94.1 2.0 %collective-permute-done.17.refs_3_ = bf16[96,384]{1,0:T(8,128)(2,1)S(1)} collective-permute-done((bf16[96,384]{1,0:T(8,128)(2,1)S(1)}, bf16[96,384]{1,0:T(8,128)(2,1)S(1)}, u32[]{:S(2)}, u32[]{:S(2)}) %collective-permute-start.17) | collective-permute-done | bytes 73760 | tf_op jit(solution)/shard_map/over_x3/ppermute | solution.py:296
  96.1 1.7 %collective-permute-start.18 = (bf16[96,384]{1,0:T(8,128)(2,1)S(1)}, bf16[96,384]{1,0:T(8,128)(2,1)S(1)}, u32[]{:S(2)}, u32[]{:S(2)}) collective-permute-start(bf16[96,384]{1,0:T(8,128)(2,1)S(1)} %four_sum_kernel.2.refs_0_), channel_id=1, source_target_pairs={{0,64},{8,72},{16,80},{24,88},{32,96},{40,104},{48,112},{56,120},{... | collective-permute-start | bytes 221192 | tf_op jit(solution)/shard_map/over_y1/ppermute | solution.py:296
  97.8 2.9 %collective-permute-start.19 = (bf16[96,384]{1,0:T(8,128)(2,1)S(1)}, bf16[96,384]{1,0:T(8,128)(2,1)S(1)}, u32[]{:S(2)}, u32[]{:S(2)}) collective-permute-start(bf16[96,384]{1,0:T(8,128)(2,1)S(1)} %four_sum_kernel.2.refs_0_), channel_id=1, source_target_pairs={{0,128},{8,136},{16,144},{24,152},{32,160},{40,168},{48,176},{56,1... | collective-permute-start | bytes 221192 | tf_op jit(solution)/shard_map/over_y2/ppermute | solution.py:296
  100.7 0.0 collective-permute-done.21
  100.7 0.2 collective-permute-start.20
  100.9 0.1 collective-permute-done.18.refs_1_
  101.0 2.8 %collective-permute-done.19.refs_2_ = bf16[96,384]{1,0:T(8,128)(2,1)S(1)} collective-permute-done((bf16[96,384]{1,0:T(8,128)(2,1)S(1)}, bf16[96,384]{1,0:T(8,128)(2,1)S(1)}, u32[]{:S(2)}, u32[]{:S(2)}) %collective-permute-start.19) | collective-permute-done | bytes 73760 | tf_op jit(solution)/shard_map/over_y2/ppermute | solution.py:296
  103.8 2.4 %collective-permute-done.20.refs_3_ = bf16[96,384]{1,0:T(8,128)(2,1)S(1)} collective-permute-done((bf16[96,384]{1,0:T(8,128)(2,1)S(1)}, bf16[96,384]{1,0:T(8,128)(2,1)S(1)}, u32[]{:S(2)}, u32[]{:S(2)}) %collective-permute-start.20) | collective-permute-done | bytes 73760 | tf_op jit(solution)/shard_map/over_y3/ppermute | solution.py:296
  106.2 0.7 copy-done.2
  107.0 5.8 %collective-permute-start.22 = (bf16[96,384]{1,0:T(8,128)(2,1)S(1)}, bf16[96,384]{1,0:T(8,128)(2,1)S(1)}, u32[]{:S(2)}, u32[]{:S(2)}) collective-permute-start(bf16[96,384]{1,0:T(8,128)(2,1)S(1)} %four_sum_kernel.3.refs_1_), channel_id=1, source_target_pairs={{0,32},{8,40},{16,48},{24,56},{32,0},{40,8},{48,16},{56,24},{64,96... | collective-permute-start | bytes 221192 | tf_op jit(solution)/shard_map/over_z/ppermute | solution.py:296
  112.7 3.1 %collective-permute-done.22.refs_2_ = bf16[96,384]{1,0:T(8,128)(2,1)S(1)} collective-permute-done((bf16[96,384]{1,0:T(8,128)(2,1)S(1)}, bf16[96,384]{1,0:T(8,128)(2,1)S(1)}, u32[]{:S(2)}, u32[]{:S(2)}) %collective-permute-start.22) | collective-permute-done | bytes 73760 | tf_op jit(solution)/shard_map/over_z/ppermute | solution.py:296
  115.9 1.5 %final_kernel.1 = (bf16[16,2,48,384]{3,2,1,0:T(8,128)(2,1)}, f32[2,48,384]{2,1,0:T(8,128)}) custom-call(s32[1]{0:T(128)} %bitcast.refs_0_, bf16[96,384]{1,0:T(8,128)(2,1)S(1)} %four_sum_kernel.3.refs_1_, bf16[96,384]{1,0:T(8,128)(2,1)S(1)} %collective-permute-done.22.refs_2_, bf16[4,4,48,384]{3,2,1,0:T(8,128)(2,1)S(1)} %get-tuple-element.42.refs_3_, ...), custom_call_target="tpu_custom_call" | custom-call | bytes 3538948 | tf_op jit(solution)/shard_map/final_kernel/pallas_call | solution.py:274
  (29 shorter events, 0.6 us)
Async XLA Ops:
  0.6 1.3 %copy-start.1 = (bf16[16,2,48,384]{3,2,1,0:T(8,128)(2,1)S(1)}, bf16[16,2,48,384]{3,2,1,0:T(8,128)(2,1)}, u32[]{:S(2)}) copy-start(bf16[16,2,48,384]{3,2,1,0:T(8,128)(2,1)} %param.5) | copy-start | bytes 3538948
  1.9 1.3 %copy-start.4 = (bf16[16,2,48,384]{3,2,1,0:T(8,128)(2,1)S(1)}, bf16[16,2,48,384]{3,2,1,0:T(8,128)(2,1)}, u32[]{:S(2)}) copy-start(bf16[16,2,48,384]{3,2,1,0:T(8,128)(2,1)} %refs_1_.2) | copy-start | bytes 3538948
  2.0 3.3 %copy-start.5 = (f32[48,384]{1,0:T(8,128)S(1)}, f32[48,384]{1,0:T(8,128)}, u32[]{:S(2)}) copy-start(f32[48,384]{1,0:T(8,128)} %param.9) | copy-start | bytes 221188
  2.0 3.4 %collective-permute-start = (bf16[4,4,48,384]{3,2,1,0:T(8,128)(2,1)S(1)}, bf16[4,4,48,384]{3,2,1,0:T(8,128)(2,1)S(1)}, u32[]{:S(2)}, u32[]{:S(2)}) collective-permute-start(bf16[4,4,48,384]{3,2,1,0:T(8,128)(2,1)S(1)} %get-tuple-element.28), channel_id=1, source_target_pairs={{0,1},{1,0},{2,3},{3,2},{4,5},{5,4},{6,7},{7,6},{8,9},{9,8},{10,11... | collective-permute-start | bytes 1769480 | tf_op jit(solution)/shard_map/forward_entry_core/ppermute | solution.py:291
  5.2 5.1 %collective-permute-start.3 = (bf16[4,4,48,384]{3,2,1,0:T(8,128)(2,1)S(1)}, bf16[4,4,48,384]{3,2,1,0:T(8,128)(2,1)S(1)}, u32[]{:S(2)}, u32[]{:S(2)}) collective-permute-start(bf16[4,4,48,384]{3,2,1,0:T(8,128)(2,1)S(1)} %get-tuple-element.29), channel_id=1, source_target_pairs={{0,1},{1,0},{2,3},{3,2},{4,5},{5,4},{6,7},{7,6},{8,9},{9,8},{10,11... | collective-permute-start | bytes 1769480 | tf_op jit(solution)/shard_map/backward_entry_core/ppermute | solution.py:291
  5.5 17.3 %copy-start = (f32[3,384,384]{2,1,0:T(8,128)S(1)}, f32[3,384,384]{2,1,0:T(8,128)}, u32[]{:S(2)}) copy-start(f32[3,384,384]{2,1,0:T(8,128)} %refs_2_.1) | copy-start | bytes 5308420
  5.5 17.3 %copy-start.3 = (s32[16]{0:T(128)S(1)}, s32[16]{0:T(128)}, u32[]{:S(2)}) copy-start(s32[16]{0:T(128)} %refs_1_.3) | copy-start | bytes 196
  5.6 17.1 %collective-permute-start.2 = (bf16[9,48,384]{2,1,0:T(8,128)(2,1)S(1)}, bf16[9,48,384]{2,1,0:T(8,128)(2,1)S(1)}, u32[]{:S(2)}, u32[]{:S(2)}) collective-permute-start(bf16[9,48,384]{2,1,0:T(8,128)(2,1)S(1)} %get-tuple-element.68), channel_id=1, source_target_pairs={{0,2},{1,3},{2,0},{3,1},{4,6},{5,7},{6,4},{7,5},{8,10},{9,11},{10,... | collective-permute-start | bytes 995336 | tf_op jit(solution)/shard_map/forward_entry_chip1/ppermute | solution.py:291
  5.9 26.1 %collective-permute-start.1 = (bf16[9,48,384]{2,1,0:T(8,128)(2,1)S(1)}, bf16[9,48,384]{2,1,0:T(8,128)(2,1)S(1)}, u32[]{:S(2)}, u32[]{:S(2)}) collective-permute-start(bf16[9,48,384]{2,1,0:T(8,128)(2,1)S(1)} %get-tuple-element.69), channel_id=1, source_target_pairs={{0,4},{1,5},{2,6},{3,7},{4,0},{5,1},{6,2},{7,3},{8,12},{9,13},{10,... | collective-permute-start | bytes 995336 | tf_op jit(solution)/shard_map/forward_entry_chip2/ppermute | solution.py:291
  9.2 27.6 %collective-permute-start.7 = (bf16[9,48,384]{2,1,0:T(8,128)(2,1)S(1)}, bf16[9,48,384]{2,1,0:T(8,128)(2,1)S(1)}, u32[]{:S(2)}, u32[]{:S(2)}) collective-permute-start(bf16[9,48,384]{2,1,0:T(8,128)(2,1)S(1)} %get-tuple-element.67), channel_id=1, source_target_pairs={{0,6},{1,7},{2,4},{3,5},{4,2},{5,3},{6,0},{7,1},{8,14},{9,15},{10,... | collective-permute-start | bytes 995336 | tf_op jit(solution)/shard_map/forward_entry_chip3/ppermute | solution.py:291
  32.1 10.8 %collective-permute-start.4 = (bf16[8,48,384]{2,1,0:T(8,128)(2,1)S(1)}, bf16[8,48,384]{2,1,0:T(8,128)(2,1)S(1)}, u32[]{:S(2)}, u32[]{:S(2)}) collective-permute-start(bf16[8,48,384]{2,1,0:T(8,128)(2,1)S(1)} %pad_maximum_fusion.3), channel_id=1, source_target_pairs={{0,2},{1,3},{2,0},{3,1},{4,6},{5,7},{6,4},{7,5},{8,10},{9,11},{10,... | collective-permute-start | bytes 884744 | tf_op jit(solution)/shard_map/backward_entry_chip1/ppermute | solution.py:291
  32.3 25.8 %collective-permute-start.5 = (bf16[8,48,384]{2,1,0:T(8,128)(2,1)S(1)}, bf16[8,48,384]{2,1,0:T(8,128)(2,1)S(1)}, u32[]{:S(2)}, u32[]{:S(2)}) collective-permute-start(bf16[8,48,384]{2,1,0:T(8,128)(2,1)S(1)} %pad_maximum_fusion.4), channel_id=1, source_target_pairs={{0,4},{1,5},{2,6},{3,7},{4,0},{5,1},{6,2},{7,3},{8,12},{9,13},{10,... | collective-permute-start | bytes 884744 | tf_op jit(solution)/shard_map/backward_entry_chip2/ppermute | solution.py:291
  35.4 22.7 %collective-permute-start.6 = (bf16[8,48,384]{2,1,0:T(8,128)(2,1)S(1)}, bf16[8,48,384]{2,1,0:T(8,128)(2,1)S(1)}, u32[]{:S(2)}, u32[]{:S(2)}) collective-permute-start(bf16[8,48,384]{2,1,0:T(8,128)(2,1)S(1)} %pad_maximum_fusion.5), channel_id=1, source_target_pairs={{0,6},{1,7},{2,4},{3,5},{4,2},{5,3},{6,0},{7,1},{8,14},{9,15},{10,... | collective-permute-start | bytes 884744 | tf_op jit(solution)/shard_map/backward_entry_chip3/ppermute | solution.py:291
  36.9 5.4 %collective-permute-start.8 = (bf16[4,48,384]{2,1,0:T(8,128)(2,1)S(1)}, bf16[4,48,384]{2,1,0:T(8,128)(2,1)S(1)}, u32[]{:S(2)}, u32[]{:S(2)}) collective-permute-start(bf16[4,48,384]{2,1,0:T(8,128)(2,1)S(1)} %pad_maximum_fusion.8.refs_1_), channel_id=1, source_target_pairs={{0,1},{1,0},{2,3},{3,2},{4,5},{5,4},{6,7},{7,6},{8,9},{9,8},{10,11... | collective-permute-start | bytes 442376 | tf_op jit(solution)/shard_map/mask_core/ppermute | solution.py:291
  41.8 28.7 %collective-permute-start.10 = (bf16[4,4,48,384]{3,2,1,0:T(8,128)(2,1)S(1)}, bf16[4,4,48,384]{3,2,1,0:T(8,128)(2,1)S(1)}, u32[]{:S(2)}, u32[]{:S(2)}) collective-permute-start(bf16[4,4,48,384]{3,2,1,0:T(8,128)(2,1)S(1)} %get-tuple-element.37), channel_id=1, source_target_pairs={{0,1},{1,0},{2,3},{3,2},{4,5},{5,4},{6,7},{7,6},{8,9},{9,8},{10,11... | collective-permute-start | bytes 1769480 | tf_op jit(solution)/shard_map/forward_exit_core/ppermute | solution.py:291
  62.7 7.8 %collective-permute-start.9 = (bf16[400,384]{1,0:T(8,128)(2,1)S(1)}, bf16[400,384]{1,0:T(8,128)(2,1)S(1)}, u32[]{:S(2)}, u32[]{:S(2)}) collective-permute-start(bf16[400,384]{1,0:T(8,128)(2,1)S(1)} %get-tuple-element.36), channel_id=1, source_target_pairs={{0,1},{1,0},{2,3},{3,2},{4,5},{5,4},{6,7},{7,6},{8,9},{9,8},{10,11... | collective-permute-start | bytes 921608 | tf_op jit(solution)/shard_map/over_core/ppermute | solution.py:291
  62.9 19.1 %collective-permute-start.14 = (bf16[4,48,384]{2,1,0:T(8,128)(2,1)S(1)}, bf16[4,48,384]{2,1,0:T(8,128)(2,1)S(1)}, u32[]{:S(2)}, u32[]{:S(2)}) collective-permute-start(bf16[4,48,384]{2,1,0:T(8,128)(2,1)S(1)} %get-tuple-element.51), channel_id=1, source_target_pairs={{0,4},{1,5},{2,6},{3,7},{4,0},{5,1},{6,2},{7,3},{8,12},{9,13},{10,... | collective-permute-start | bytes 442376 | tf_op jit(solution)/shard_map/forward_exit_start2/ppermute | solution.py:291
  70.6 11.4 %collective-permute-start.11 = (bf16[112,384]{1,0:T(8,128)(2,1)S(1)}, bf16[112,384]{1,0:T(8,128)(2,1)S(1)}, u32[]{:S(2)}, u32[]{:S(2)}) collective-permute-start(bf16[112,384]{1,0:T(8,128)(2,1)S(1)} %get-tuple-element.39), channel_id=1, source_target_pairs={{0,2},{1,3},{2,0},{3,1},{4,6},{5,7},{6,4},{7,5},{8,10},{9,11},{10,... | collective-permute-start | bytes 258056 | tf_op jit(solution)/shard_map/over_chip1/ppermute | solution.py:291
  71.0 12.8 %collective-permute-start.12 = (bf16[112,384]{1,0:T(8,128)(2,1)S(1)}, bf16[112,384]{1,0:T(8,128)(2,1)S(1)}, u32[]{:S(2)}, u32[]{:S(2)}) collective-permute-start(bf16[112,384]{1,0:T(8,128)(2,1)S(1)} %get-tuple-element.40), channel_id=1, source_target_pairs={{0,4},{1,5},{2,6},{3,7},{4,0},{5,1},{6,2},{7,3},{8,12},{9,13},{10,... | collective-permute-start | bytes 258056 | tf_op jit(solution)/shard_map/over_chip2/ppermute | solution.py:291
  72.6 11.2 %collective-permute-start.13 = (bf16[112,384]{1,0:T(8,128)(2,1)S(1)}, bf16[112,384]{1,0:T(8,128)(2,1)S(1)}, u32[]{:S(2)}, u32[]{:S(2)}) collective-permute-start(bf16[112,384]{1,0:T(8,128)(2,1)S(1)} %get-tuple-element.41), channel_id=1, source_target_pairs={{0,6},{1,7},{2,4},{3,5},{4,2},{5,3},{6,0},{7,1},{8,14},{9,15},{10,... | collective-permute-start | bytes 258056 | tf_op jit(solution)/shard_map/over_chip3/ppermute | solution.py:291
  83.9 7.2 %collective-permute-start.15 = (bf16[96,384]{1,0:T(8,128)(2,1)S(1)}, bf16[96,384]{1,0:T(8,128)(2,1)S(1)}, u32[]{:S(2)}, u32[]{:S(2)}) collective-permute-start(bf16[96,384]{1,0:T(8,128)(2,1)S(1)} %get-tuple-element.43.refs_0_), channel_id=1, source_target_pairs={{0,8},{8,0},{16,24},{24,16},{32,40},{40,32},{48,56},{56,48},{64,72... | collective-permute-start | bytes 221192 | tf_op jit(solution)/shard_map/over_x1/ppermute | solution.py:296
  85.7 15.0 %collective-permute-start.21 = (bf16[4,48,384]{2,1,0:T(8,128)(2,1)S(1)}, bf16[4,48,384]{2,1,0:T(8,128)(2,1)S(1)}, u32[]{:S(2)}, u32[]{:S(2)}) collective-permute-start(bf16[4,48,384]{2,1,0:T(8,128)(2,1)S(1)} %get-tuple-element.44), channel_id=1, source_target_pairs={{0,4},{1,5},{2,6},{3,7},{4,0},{5,1},{6,2},{7,3},{8,12},{9,13},{10,... | collective-permute-start | bytes 442376 | tf_op jit(solution)/shard_map/forward_exit_chip2/ppermute | solution.py:291
  87.8 6.3 %collective-permute-start.16 = (bf16[96,384]{1,0:T(8,128)(2,1)S(1)}, bf16[96,384]{1,0:T(8,128)(2,1)S(1)}, u32[]{:S(2)}, u32[]{:S(2)}) collective-permute-start(bf16[96,384]{1,0:T(8,128)(2,1)S(1)} %get-tuple-element.43.refs_0_), channel_id=1, source_target_pairs={{0,16},{8,24},{16,0},{24,8},{32,48},{40,56},{48,32},{56,40},{64,80... | collective-permute-start | bytes 221192 | tf_op jit(solution)/shard_map/over_x2/ppermute | solution.py:296
  90.5 5.6 %collective-permute-start.17 = (bf16[96,384]{1,0:T(8,128)(2,1)S(1)}, bf16[96,384]{1,0:T(8,128)(2,1)S(1)}, u32[]{:S(2)}, u32[]{:S(2)}) collective-permute-start(bf16[96,384]{1,0:T(8,128)(2,1)S(1)} %get-tuple-element.43.refs_0_), channel_id=1, source_target_pairs={{0,24},{8,16},{16,8},{24,0},{32,56},{40,48},{48,40},{56,32},{64,88... | collective-permute-start | bytes 221192 | tf_op jit(solution)/shard_map/over_x3/ppermute | solution.py:296
  91.0 24.9 %collective-permute-start.23 = (bf16[8,48,384]{2,1,0:T(8,128)(2,1)S(1)}, bf16[8,48,384]{2,1,0:T(8,128)(2,1)S(1)}, u32[]{:S(2)}, u32[]{:S(2)}) collective-permute-start(bf16[8,48,384]{2,1,0:T(8,128)(2,1)S(1)} %get-tuple-element.45), channel_id=1, source_target_pairs={{0,2},{1,3},{2,0},{3,1},{4,6},{5,7},{6,4},{7,5},{8,10},{9,11},{10,... | collective-permute-start | bytes 884744 | tf_op jit(solution)/shard_map/forward_exit_chip1/ppermute | solution.py:291
  91.1 24.8 %collective-permute-start.24 = (bf16[8,48,384]{2,1,0:T(8,128)(2,1)S(1)}, bf16[8,48,384]{2,1,0:T(8,128)(2,1)S(1)}, u32[]{:S(2)}, u32[]{:S(2)}) collective-permute-start(bf16[8,48,384]{2,1,0:T(8,128)(2,1)S(1)} %get-tuple-element.46), channel_id=1, source_target_pairs={{0,6},{1,7},{2,4},{3,5},{4,2},{5,3},{6,0},{7,1},{8,14},{9,15},{10,... | collective-permute-start | bytes 884744 | tf_op jit(solution)/shard_map/forward_exit_chip3/ppermute | solution.py:291
  96.1 4.9 %collective-permute-start.18 = (bf16[96,384]{1,0:T(8,128)(2,1)S(1)}, bf16[96,384]{1,0:T(8,128)(2,1)S(1)}, u32[]{:S(2)}, u32[]{:S(2)}) collective-permute-start(bf16[96,384]{1,0:T(8,128)(2,1)S(1)} %four_sum_kernel.2.refs_0_), channel_id=1, source_target_pairs={{0,64},{8,72},{16,80},{24,88},{32,96},{40,104},{48,112},{56,120},{... | collective-permute-start | bytes 221192 | tf_op jit(solution)/shard_map/over_y1/ppermute | solution.py:296
  97.8 6.0 %collective-permute-start.19 = (bf16[96,384]{1,0:T(8,128)(2,1)S(1)}, bf16[96,384]{1,0:T(8,128)(2,1)S(1)}, u32[]{:S(2)}, u32[]{:S(2)}) collective-permute-start(bf16[96,384]{1,0:T(8,128)(2,1)S(1)} %four_sum_kernel.2.refs_0_), channel_id=1, source_target_pairs={{0,128},{8,136},{16,144},{24,152},{32,160},{40,168},{48,176},{56,1... | collective-permute-start | bytes 221192 | tf_op jit(solution)/shard_map/over_y2/ppermute | solution.py:296
  100.7 5.6 %collective-permute-start.20 = (bf16[96,384]{1,0:T(8,128)(2,1)S(1)}, bf16[96,384]{1,0:T(8,128)(2,1)S(1)}, u32[]{:S(2)}, u32[]{:S(2)}) collective-permute-start(bf16[96,384]{1,0:T(8,128)(2,1)S(1)} %four_sum_kernel.2.refs_0_), channel_id=1, source_target_pairs={{0,192},{8,200},{16,208},{24,216},{32,224},{40,232},{48,240},{56,2... | collective-permute-start | bytes 221192 | tf_op jit(solution)/shard_map/over_y3/ppermute | solution.py:296
  106.2 0.7 copy-start.2
  107.0 8.9 %collective-permute-start.22 = (bf16[96,384]{1,0:T(8,128)(2,1)S(1)}, bf16[96,384]{1,0:T(8,128)(2,1)S(1)}, u32[]{:S(2)}, u32[]{:S(2)}) collective-permute-start(bf16[96,384]{1,0:T(8,128)(2,1)S(1)} %four_sum_kernel.3.refs_1_), channel_id=1, source_target_pairs={{0,32},{8,40},{16,48},{24,56},{32,0},{40,8},{48,16},{56,24},{64,96... | collective-permute-start | bytes 221192 | tf_op jit(solution)/shard_map/over_z/ppermute | solution.py:296

commit v3 on v1

--- a/solution.py
+++ b/solution.py
@@ -19,7 +19,7 @@
 SMEM = pl.BlockSpec(memory_space=pltpu.SMEM)
 VMEM = pl.BlockSpec(memory_space=pltpu.VMEM)
 ANY = pl.BlockSpec(memory_space=pl.ANY)
-LIMIT = 24 * 1024 * 1024
+LIMIT = 16 * 1024 * 1024
 BF16, F32 = jnp.bfloat16, jnp.float32
 
 

time: 117 us -> 117 us (level)
  no operation moved by 1% of the time
where the time goes in v3:
time: 117 us
  waiting for transfers between devices  54.9 us (47%)
  starting transfers between devices  42.2 us (36%)
  Pallas kernels  15.9 us (14%)
  local copies, waits for them, and re-layouts  2.67 us (2%)
    ppermute x18, waiting for transfers between devices, over_rows(): return lax.ppermute(block, 'rows', [(s, s ^ k) for s in range(ROWS)])  43.9 us
    ppermute x18, starting transfers between devices, over_rows(): return lax.ppermute(block, 'rows', [(s, s ^ k) for s in range(ROWS)])  26.9 us
    pallas_call x12, Pallas kernels, call(): pl.pallas_call(body, name=kernel.__name__, out_shape=[jax.ShapeDtypeStruc...  15.9 us
    ppermute x7, starting transfers between devices, over_modes(): lax.ppermute(block, 'modes', [(s, s ^ k) for s in range(lax.axis_size('mo...  15.3 us
    ppermute x7, waiting for transfers between devices, over_modes(): lax.ppermute(block, 'modes', [(s, s ^ k) for s in range(lax.axis_size('mo...  11 us
    unnamed x11, local copies, waits for them, and re-layouts  2.35 us
  transfers between devices with their start and end apart: 25, of which 11 were waited for; matrix products, arithmetic and copies ran while one was open for 1% of the time, Pallas kernels for 12%

profile of v3, /device:TPU:0, one launch (start us, length us, event | category | flops | bytes accessed | tf_op | source)
XLA Modules:
  0.0 116.9 jit_solution(6055472239795515045)
XLA Ops:
  0.6 1.3 %copy-done.1 = bf16[16,2,48,384]{3,2,1,0:T(8,128)(2,1)S(1)} copy-done((bf16[16,2,48,384]{3,2,1,0:T(8,128)(2,1)S(1)}, bf16[16,2,48,384]{3,2,1,0:T(8,128)(2,1)}, u32[]{:S(2)}) %copy-start.1) | copy-done | bytes 1179672
  1.9 0.1 cut_kernel.1
  2.0 0.0 copy-start.4
  2.0 0.1 collective-permute-start
  2.1 1.1 copy-done.3
  3.2 2.0 %tables_kernel.1 = (bf16[768,768]{1,0:T(8,128)(2,1)S(1)}, bf16[768,768]{1,0:T(8,128)(2,1)S(1)}, bf16[4,4,48,384]{3,2,1,0:T(8,128)(2,1)S(1)}, bf16[4,4,48,384]{3,2,1,0:T(8,128)(2,1)S(1)}) custom-call(s32[1]{0:T(128)} %bitcast.refs_0_, bf16[16,2,48,384]{3,2,1,0:T(8,128)(2,1)S(1)} %copy-done.3), custom_call_target="tpu_custom_call" | custom-call | flops 905969664 | bytes 4718596 | tf_op jit(solution)/shard_map/tables_kernel/pallas_call | solution.py:271
  5.2 0.1 collective-permute-start.3
  5.4 0.0 collective-permute-done.refs_2_
  5.5 0.0 copy-start
  5.5 0.0 copy-start.2
  5.5 0.2 pad_maximum_fusion
  5.6 0.3 collective-permute-start.2
  5.9 3.3 %collective-permute-start.1 = (bf16[9,48,384]{2,1,0:T(8,128)(2,1)S(1)}, bf16[9,48,384]{2,1,0:T(8,128)(2,1)S(1)}, u32[]{:S(2)}, u32[]{:S(2)}) collective-permute-start(bf16[9,48,384]{2,1,0:T(8,128)(2,1)S(1)} %get-tuple-element.71), channel_id=1, source_target_pairs={{0,4},{1,5},{2,6},{3,7},{4,0},{5,1},{6,2},{7,3},{8,12},{9,13},{10,... | collective-permute-start | bytes 995336 | tf_op jit(solution)/shard_map/forward_entry_chip2/ppermute | solution.py:288
  9.2 1.0 collective-permute-start.7
  10.3 0.0 collective-permute-done.3.refs_4_
  10.3 12.5 %collective-permute-done.2.refs_3_ = bf16[9,48,384]{2,1,0:T(8,128)(2,1)S(1)} collective-permute-done((bf16[9,48,384]{2,1,0:T(8,128)(2,1)S(1)}, bf16[9,48,384]{2,1,0:T(8,128)(2,1)S(1)}, u32[]{:S(2)}, u32[]{:S(2)}) %collective-permute-start.2) | collective-permute-done | bytes 331808 | tf_op jit(solution)/shard_map/forward_entry_chip1/ppermute | solution.py:288
  22.7 1.7 %trig_kernel.1 = (f32[2,2,384,384]{3,2,1,0:T(8,128)S(1)}, bf16[4,4,48,384]{3,2,1,0:T(8,128)(2,1)S(1)}) custom-call(s32[1]{0:T(128)} %bitcast.refs_0_, s32[16]{0:T(128)S(1)} %copy-done.2, f32[3,384,384]{2,1,0:T(8,128)S(1)} %copy-done, bf16[9,48,384]{2,1,0:T(8,128)(2,1)S(1)} %collective-permute-done.2.refs_3_, ...), custom_call_target="tpu_custom_call", output_to_operand_aliasing={{1}: (4, {})} | custom-call | bytes 4128836 | tf_op jit(solution)/shard_map/trig_kernel/pallas_call | solution.py:271
  24.5 7.6 %collective-permute-done.1.refs_1_.refs_4_ = bf16[9,48,384]{2,1,0:T(8,128)(2,1)S(1)} collective-permute-done((bf16[9,48,384]{2,1,0:T(8,128)(2,1)S(1)}, bf16[9,48,384]{2,1,0:T(8,128)(2,1)S(1)}, u32[]{:S(2)}, u32[]{:S(2)}) %collective-permute-start.1) | collective-permute-done | bytes 331808 | tf_op jit(solution)/shard_map/forward_entry_chip2/ppermute | solution.py:288
  32.1 0.1 collective-permute-start.4
  32.3 3.1 %collective-permute-start.5 = (bf16[8,48,384]{2,1,0:T(8,128)(2,1)S(1)}, bf16[8,48,384]{2,1,0:T(8,128)(2,1)S(1)}, u32[]{:S(2)}, u32[]{:S(2)}) collective-permute-start(bf16[8,48,384]{2,1,0:T(8,128)(2,1)S(1)} %pad_maximum_fusion.4), channel_id=1, source_target_pairs={{0,4},{1,5},{2,6},{3,7},{4,0},{5,1},{6,2},{7,3},{8,12},{9,13},{10,... | collective-permute-start | bytes 884744 | tf_op jit(solution)/shard_map/backward_entry_chip2/ppermute | solution.py:288
  35.4 1.4 %collective-permute-start.6 = (bf16[8,48,384]{2,1,0:T(8,128)(2,1)S(1)}, bf16[8,48,384]{2,1,0:T(8,128)(2,1)S(1)}, u32[]{:S(2)}, u32[]{:S(2)}) collective-permute-start(bf16[8,48,384]{2,1,0:T(8,128)(2,1)S(1)} %pad_maximum_fusion.5), channel_id=1, source_target_pairs={{0,6},{1,7},{2,4},{3,5},{4,2},{5,3},{6,0},{7,1},{8,14},{9,15},{10,... | collective-permute-start | bytes 884744 | tf_op jit(solution)/shard_map/backward_entry_chip3/ppermute | solution.py:288
  36.9 0.0 collective-permute-done.7.refs_5_
  36.9 0.3 collective-permute-start.8
  37.2 4.5 %forward_kernel.1 = (f32[2,384,768]{2,1,0:T(8,128)S(1)}, bf16[4,4,48,384]{3,2,1,0:T(8,128)(2,1)S(1)}, bf16[4,4,48,384]{3,2,1,0:T(8,128)(2,1)S(1)}) custom-call(s32[1]{0:T(128)} %bitcast.refs_0_, bf16[4,4,48,384]{3,2,1,0:T(8,128)(2,1)S(1)} %get-tuple-element.28.refs_1_, bf16[4,4,48,384]{3,2,1,0:T(8,128)(2,1)S(1)} %collective-permute-done.refs_2_, ...), custom_call_target="tpu_custom_call" | custom-call | flops 3623878656 | bytes 10432516 | tf_op jit(solution)/shard_map/forward_kernel/pallas_call | solution.py:271
  41.8 0.6 collective-permute-start.10
  42.3 0.0 collective-permute-done.8.refs_2_
  42.3 0.6 mask_kernel.1.refs_10_
  42.9 0.0 collective-permute-done.4.refs_3_
  42.9 15.2 %collective-permute-done.5.refs_4_ = bf16[8,48,384]{2,1,0:T(8,128)(2,1)S(1)} collective-permute-done((bf16[8,48,384]{2,1,0:T(8,128)(2,1)S(1)}, bf16[8,48,384]{2,1,0:T(8,128)(2,1)S(1)}, u32[]{:S(2)}, u32[]{:S(2)}) %collective-permute-start.5) | collective-permute-done | bytes 294944 | tf_op jit(solution)/shard_map/backward_entry_chip2/ppermute | solution.py:288
  58.1 4.6 %backward_kernel.1 = (bf16[400,384]{1,0:T(8,128)(2,1)S(1)}, bf16[400,384]{1,0:T(8,128)(2,1)S(1)}) custom-call(s32[1]{0:T(128)} %bitcast.refs_0_, bf16[4,4,48,384]{3,2,1,0:T(8,128)(2,1)S(1)} %get-tuple-element.27.refs_1_, bf16[4,4,48,384]{3,2,1,0:T(8,128)(2,1)S(1)} %gate_kernel.1.refs_2_, bf16[8,48,384]{2,1,0:T(8,128)(2,1)S(1)} %collective-permute-done.4.refs_3_, ...), custom_call_target="tpu_custom_call" | custom-call | flops 2717908992 | bytes 10936324 | tf_op jit(solution)/shard_map/backward_kernel/pallas_call | solution.py:271
  62.7 0.1 collective-permute-start.9
  62.9 7.6 %collective-permute-start.14 = (bf16[4,48,384]{2,1,0:T(8,128)(2,1)S(1)}, bf16[4,48,384]{2,1,0:T(8,128)(2,1)S(1)}, u32[]{:S(2)}, u32[]{:S(2)}) collective-permute-start(bf16[4,48,384]{2,1,0:T(8,128)(2,1)S(1)} %get-tuple-element.53), channel_id=1, source_target_pairs={{0,4},{1,5},{2,6},{3,7},{4,0},{5,1},{6,2},{7,3},{8,12},{9,13},{10,... | collective-permute-start | bytes 442376 | tf_op jit(solution)/shard_map/forward_exit_start2/ppermute | solution.py:288
  70.5 0.0 collective-permute-done.9.refs_1_
  70.5 0.1 core_sum_kernel.1
  70.6 0.5 collective-permute-start.11
  71.0 1.5 %collective-permute-start.12 = (bf16[112,384]{1,0:T(8,128)(2,1)S(1)}, bf16[112,384]{1,0:T(8,128)(2,1)S(1)}, u32[]{:S(2)}, u32[]{:S(2)}) collective-permute-start(bf16[112,384]{1,0:T(8,128)(2,1)S(1)} %get-tuple-element.41), channel_id=1, source_target_pairs={{0,4},{1,5},{2,6},{3,7},{4,0},{5,1},{6,2},{7,3},{8,12},{9,13},{10,... | collective-permute-start | bytes 258056 | tf_op jit(solution)/shard_map/over_chip2/ppermute | solution.py:288
  72.6 2.5 %collective-permute-start.13 = (bf16[112,384]{1,0:T(8,128)(2,1)S(1)}, bf16[112,384]{1,0:T(8,128)(2,1)S(1)}, u32[]{:S(2)}, u32[]{:S(2)}) collective-permute-start(bf16[112,384]{1,0:T(8,128)(2,1)S(1)} %get-tuple-element.42), channel_id=1, source_target_pairs={{0,6},{1,7},{2,4},{3,5},{4,2},{5,3},{6,0},{7,1},{8,14},{9,15},{10,... | collective-permute-start | bytes 258056 | tf_op jit(solution)/shard_map/over_chip3/ppermute | solution.py:288
  75.0 0.1 pad_maximum_fusion.6
  75.1 6.9 %collective-permute-done.14.refs_5_ = bf16[4,48,384]{2,1,0:T(8,128)(2,1)S(1)} collective-permute-done((bf16[4,48,384]{2,1,0:T(8,128)(2,1)S(1)}, bf16[4,48,384]{2,1,0:T(8,128)(2,1)S(1)}, u32[]{:S(2)}, u32[]{:S(2)}) %collective-permute-start.14) | collective-permute-done | bytes 147488 | tf_op jit(solution)/shard_map/forward_exit_start2/ppermute | solution.py:288
  82.0 0.0 collective-permute-done.11.refs_2_
  82.0 1.8 %collective-permute-done.12.refs_3_ = bf16[112,384]{1,0:T(8,128)(2,1)S(1)} collective-permute-done((bf16[112,384]{1,0:T(8,128)(2,1)S(1)}, bf16[112,384]{1,0:T(8,128)(2,1)S(1)}, u32[]{:S(2)}, u32[]{:S(2)}) %collective-permute-start.12) | collective-permute-done | bytes 86048 | tf_op jit(solution)/shard_map/over_chip2/ppermute | solution.py:288
  83.8 0.0 collective-permute-done.13.refs_4_
  83.8 0.6 chip_sum_kernel.1
  84.4 1.5 %collective-permute-start.15 = (bf16[96,384]{1,0:T(8,128)(2,1)S(1)}, bf16[96,384]{1,0:T(8,128)(2,1)S(1)}, u32[]{:S(2)}, u32[]{:S(2)}) collective-permute-start(bf16[96,384]{1,0:T(8,128)(2,1)S(1)} %get-tuple-element.44.refs_0_), channel_id=1, source_target_pairs={{0,8},{8,0},{16,24},{24,16},{32,40},{40,32},{48,56},{56,48},{64,72... | collective-permute-start | bytes 221192 | tf_op jit(solution)/shard_map/over_x1/ppermute | solution.py:293
  85.9 2.1 %collective-permute-start.21 = (bf16[4,48,384]{2,1,0:T(8,128)(2,1)S(1)}, bf16[4,48,384]{2,1,0:T(8,128)(2,1)S(1)}, u32[]{:S(2)}, u32[]{:S(2)}) collective-permute-start(bf16[4,48,384]{2,1,0:T(8,128)(2,1)S(1)} %get-tuple-element.45), channel_id=1, source_target_pairs={{0,4},{1,5},{2,6},{3,7},{4,0},{5,1},{6,2},{7,3},{8,12},{9,13},{10,... | collective-permute-start | bytes 442376 | tf_op jit(solution)/shard_map/forward_exit_chip2/ppermute | solution.py:288
  88.0 2.7 %collective-permute-start.16 = (bf16[96,384]{1,0:T(8,128)(2,1)S(1)}, bf16[96,384]{1,0:T(8,128)(2,1)S(1)}, u32[]{:S(2)}, u32[]{:S(2)}) collective-permute-start(bf16[96,384]{1,0:T(8,128)(2,1)S(1)} %get-tuple-element.44.refs_0_), channel_id=1, source_target_pairs={{0,16},{8,24},{16,0},{24,8},{32,48},{40,56},{48,32},{56,40},{64,80... | collective-permute-start | bytes 221192 | tf_op jit(solution)/shard_map/over_x2/ppermute | solution.py:293
  90.7 0.5 collective-permute-start.17
  91.2 0.1 collective-permute-start.23
  91.3 0.0 collective-permute-done.15.refs_1_
  91.3 2.4 %collective-permute-start.24 = (bf16[8,48,384]{2,1,0:T(8,128)(2,1)S(1)}, bf16[8,48,384]{2,1,0:T(8,128)(2,1)S(1)}, u32[]{:S(2)}, u32[]{:S(2)}) collective-permute-start(bf16[8,48,384]{2,1,0:T(8,128)(2,1)S(1)} %get-tuple-element.47), channel_id=1, source_target_pairs={{0,6},{1,7},{2,4},{3,5},{4,2},{5,3},{6,0},{7,1},{8,14},{9,15},{10,... | collective-permute-start | bytes 884744 | tf_op jit(solution)/shard_map/forward_exit_chip3/ppermute | solution.py:288
  93.7 0.2 collective-permute-done.16.refs_2_
  93.9 2.4 %collective-permute-done.17.refs_3_ = bf16[96,384]{1,0:T(8,128)(2,1)S(1)} collective-permute-done((bf16[96,384]{1,0:T(8,128)(2,1)S(1)}, bf16[96,384]{1,0:T(8,128)(2,1)S(1)}, u32[]{:S(2)}, u32[]{:S(2)}) %collective-permute-start.17) | collective-permute-done | bytes 73760 | tf_op jit(solution)/shard_map/over_x3/ppermute | solution.py:293
  96.3 1.7 %collective-permute-start.18 = (bf16[96,384]{1,0:T(8,128)(2,1)S(1)}, bf16[96,384]{1,0:T(8,128)(2,1)S(1)}, u32[]{:S(2)}, u32[]{:S(2)}) collective-permute-start(bf16[96,384]{1,0:T(8,128)(2,1)S(1)} %four_sum_kernel.2.refs_0_), channel_id=1, source_target_pairs={{0,64},{8,72},{16,80},{24,88},{32,96},{40,104},{48,112},{56,120},{... | collective-permute-start | bytes 221192 | tf_op jit(solution)/shard_map/over_y1/ppermute | solution.py:293
  98.0 2.9 %collective-permute-start.19 = (bf16[96,384]{1,0:T(8,128)(2,1)S(1)}, bf16[96,384]{1,0:T(8,128)(2,1)S(1)}, u32[]{:S(2)}, u32[]{:S(2)}) collective-permute-start(bf16[96,384]{1,0:T(8,128)(2,1)S(1)} %four_sum_kernel.2.refs_0_), channel_id=1, source_target_pairs={{0,128},{8,136},{16,144},{24,152},{32,160},{40,168},{48,176},{56,1... | collective-permute-start | bytes 221192 | tf_op jit(solution)/shard_map/over_y2/ppermute | solution.py:293
  100.9 0.0 collective-permute-done.21
  100.9 0.2 collective-permute-start.20
  101.2 0.1 collective-permute-done.18.refs_1_
  101.2 2.8 %collective-permute-done.19.refs_2_ = bf16[96,384]{1,0:T(8,128)(2,1)S(1)} collective-permute-done((bf16[96,384]{1,0:T(8,128)(2,1)S(1)}, bf16[96,384]{1,0:T(8,128)(2,1)S(1)}, u32[]{:S(2)}, u32[]{:S(2)}) %collective-permute-start.19) | collective-permute-done | bytes 73760 | tf_op jit(solution)/shard_map/over_y2/ppermute | solution.py:293
  104.0 2.4 %collective-permute-done.20.refs_3_ = bf16[96,384]{1,0:T(8,128)(2,1)S(1)} collective-permute-done((bf16[96,384]{1,0:T(8,128)(2,1)S(1)}, bf16[96,384]{1,0:T(8,128)(2,1)S(1)}, u32[]{:S(2)}, u32[]{:S(2)}) %collective-permute-start.20) | collective-permute-done | bytes 73760 | tf_op jit(solution)/shard_map/over_y3/ppermute | solution.py:293
  106.5 5.8 %collective-permute-start.22 = (bf16[96,384]{1,0:T(8,128)(2,1)S(1)}, bf16[96,384]{1,0:T(8,128)(2,1)S(1)}, u32[]{:S(2)}, u32[]{:S(2)}) collective-permute-start(bf16[96,384]{1,0:T(8,128)(2,1)S(1)} %four_sum_kernel.3.refs_1_), channel_id=1, source_target_pairs={{0,32},{8,40},{16,48},{24,56},{32,0},{40,8},{48,16},{56,24},{64,96... | collective-permute-start | bytes 221192 | tf_op jit(solution)/shard_map/over_z/ppermute | solution.py:293
  112.3 3.1 %collective-permute-done.22.refs_2_ = bf16[96,384]{1,0:T(8,128)(2,1)S(1)} collective-permute-done((bf16[96,384]{1,0:T(8,128)(2,1)S(1)}, bf16[96,384]{1,0:T(8,128)(2,1)S(1)}, u32[]{:S(2)}, u32[]{:S(2)}) %collective-permute-start.22) | collective-permute-done | bytes 73760 | tf_op jit(solution)/shard_map/over_z/ppermute | solution.py:293
  115.4 0.0 collective-permute-done.23.refs_5_
  115.4 0.0 collective-permute-done.24.refs_7_
  115.4 1.5 %final_kernel.1 = (bf16[16,2,48,384]{3,2,1,0:T(8,128)(2,1)}, f32[2,48,384]{2,1,0:T(8,128)}) custom-call(s32[1]{0:T(128)} %bitcast.refs_0_, bf16[96,384]{1,0:T(8,128)(2,1)S(1)} %four_sum_kernel.3.refs_1_, bf16[96,384]{1,0:T(8,128)(2,1)S(1)} %collective-permute-done.22.refs_2_, bf16[4,4,48,384]{3,2,1,0:T(8,128)(2,1)S(1)} %get-tuple-element.43.refs_3_, ...), custom_call_target="tpu_custom_call" | custom-call | bytes 3538948 | tf_op jit(solution)/shard_map/final_kernel/pallas_call | solution.py:271
  (26 shorter events, 0.6 us)
Async XLA Ops:
  0.6 1.3 %copy-start.1 = (bf16[16,2,48,384]{3,2,1,0:T(8,128)(2,1)S(1)}, bf16[16,2,48,384]{3,2,1,0:T(8,128)(2,1)}, u32[]{:S(2)}) copy-start(bf16[16,2,48,384]{3,2,1,0:T(8,128)(2,1)} %param.5) | copy-start | bytes 3538948
  1.9 1.3 %copy-start.3 = (bf16[16,2,48,384]{3,2,1,0:T(8,128)(2,1)S(1)}, bf16[16,2,48,384]{3,2,1,0:T(8,128)(2,1)}, u32[]{:S(2)}) copy-start(bf16[16,2,48,384]{3,2,1,0:T(8,128)(2,1)} %refs_1_.2) | copy-start | bytes 3538948
  2.0 3.3 %copy-start.4 = (f32[48,384]{1,0:T(8,128)S(1)}, f32[48,384]{1,0:T(8,128)}, u32[]{:S(2)}) copy-start(f32[48,384]{1,0:T(8,128)} %param.9) | copy-start | bytes 221188
  2.0 3.4 %collective-permute-start = (bf16[4,4,48,384]{3,2,1,0:T(8,128)(2,1)S(1)}, bf16[4,4,48,384]{3,2,1,0:T(8,128)(2,1)S(1)}, u32[]{:S(2)}, u32[]{:S(2)}) collective-permute-start(bf16[4,4,48,384]{3,2,1,0:T(8,128)(2,1)S(1)} %get-tuple-element.29), channel_id=1, source_target_pairs={{0,1},{1,0},{2,3},{3,2},{4,5},{5,4},{6,7},{7,6},{8,9},{9,8},{10,11... | collective-permute-start | bytes 1769480 | tf_op jit(solution)/shard_map/forward_entry_core/ppermute | solution.py:288
  5.2 5.1 %collective-permute-start.3 = (bf16[4,4,48,384]{3,2,1,0:T(8,128)(2,1)S(1)}, bf16[4,4,48,384]{3,2,1,0:T(8,128)(2,1)S(1)}, u32[]{:S(2)}, u32[]{:S(2)}) collective-permute-start(bf16[4,4,48,384]{3,2,1,0:T(8,128)(2,1)S(1)} %get-tuple-element.30), channel_id=1, source_target_pairs={{0,1},{1,0},{2,3},{3,2},{4,5},{5,4},{6,7},{7,6},{8,9},{9,8},{10,11... | collective-permute-start | bytes 1769480 | tf_op jit(solution)/shard_map/backward_entry_core/ppermute | solution.py:288
  5.5 17.3 %copy-start = (f32[3,384,384]{2,1,0:T(8,128)S(1)}, f32[3,384,384]{2,1,0:T(8,128)}, u32[]{:S(2)}) copy-start(f32[3,384,384]{2,1,0:T(8,128)} %refs_2_.1) | copy-start | bytes 5308420
  5.5 17.3 %copy-start.2 = (s32[16]{0:T(128)S(1)}, s32[16]{0:T(128)}, u32[]{:S(2)}) copy-start(s32[16]{0:T(128)} %refs_1_.3) | copy-start | bytes 196
  5.6 17.1 %collective-permute-start.2 = (bf16[9,48,384]{2,1,0:T(8,128)(2,1)S(1)}, bf16[9,48,384]{2,1,0:T(8,128)(2,1)S(1)}, u32[]{:S(2)}, u32[]{:S(2)}) collective-permute-start(bf16[9,48,384]{2,1,0:T(8,128)(2,1)S(1)} %get-tuple-element.70), channel_id=1, source_target_pairs={{0,2},{1,3},{2,0},{3,1},{4,6},{5,7},{6,4},{7,5},{8,10},{9,11},{10,... | collective-permute-start | bytes 995336 | tf_op jit(solution)/shard_map/forward_entry_chip1/ppermute | solution.py:288
  5.9 26.1 %collective-permute-start.1 = (bf16[9,48,384]{2,1,0:T(8,128)(2,1)S(1)}, bf16[9,48,384]{2,1,0:T(8,128)(2,1)S(1)}, u32[]{:S(2)}, u32[]{:S(2)}) collective-permute-start(bf16[9,48,384]{2,1,0:T(8,128)(2,1)S(1)} %get-tuple-element.71), channel_id=1, source_target_pairs={{0,4},{1,5},{2,6},{3,7},{4,0},{5,1},{6,2},{7,3},{8,12},{9,13},{10,... | collective-permute-start | bytes 995336 | tf_op jit(solution)/shard_map/forward_entry_chip2/ppermute | solution.py:288
  9.2 27.6 %collective-permute-start.7 = (bf16[9,48,384]{2,1,0:T(8,128)(2,1)S(1)}, bf16[9,48,384]{2,1,0:T(8,128)(2,1)S(1)}, u32[]{:S(2)}, u32[]{:S(2)}) collective-permute-start(bf16[9,48,384]{2,1,0:T(8,128)(2,1)S(1)} %get-tuple-element.69), channel_id=1, source_target_pairs={{0,6},{1,7},{2,4},{3,5},{4,2},{5,3},{6,0},{7,1},{8,14},{9,15},{10,... | collective-permute-start | bytes 995336 | tf_op jit(solution)/shard_map/forward_entry_chip3/ppermute | solution.py:288
  32.1 10.8 %collective-permute-start.4 = (bf16[8,48,384]{2,1,0:T(8,128)(2,1)S(1)}, bf16[8,48,384]{2,1,0:T(8,128)(2,1)S(1)}, u32[]{:S(2)}, u32[]{:S(2)}) collective-permute-start(bf16[8,48,384]{2,1,0:T(8,128)(2,1)S(1)} %pad_maximum_fusion.3), channel_id=1, source_target_pairs={{0,2},{1,3},{2,0},{3,1},{4,6},{5,7},{6,4},{7,5},{8,10},{9,11},{10,... | collective-permute-start | bytes 884744 | tf_op jit(solution)/shard_map/backward_entry_chip1/ppermute | solution.py:288
  32.3 25.8 %collective-permute-start.5 = (bf16[8,48,384]{2,1,0:T(8,128)(2,1)S(1)}, bf16[8,48,384]{2,1,0:T(8,128)(2,1)S(1)}, u32[]{:S(2)}, u32[]{:S(2)}) collective-permute-start(bf16[8,48,384]{2,1,0:T(8,128)(2,1)S(1)} %pad_maximum_fusion.4), channel_id=1, source_target_pairs={{0,4},{1,5},{2,6},{3,7},{4,0},{5,1},{6,2},{7,3},{8,12},{9,13},{10,... | collective-permute-start | bytes 884744 | tf_op jit(solution)/shard_map/backward_entry_chip2/ppermute | solution.py:288
  35.4 22.7 %collective-permute-start.6 = (bf16[8,48,384]{2,1,0:T(8,128)(2,1)S(1)}, bf16[8,48,384]{2,1,0:T(8,128)(2,1)S(1)}, u32[]{:S(2)}, u32[]{:S(2)}) collective-permute-start(bf16[8,48,384]{2,1,0:T(8,128)(2,1)S(1)} %pad_maximum_fusion.5), channel_id=1, source_target_pairs={{0,6},{1,7},{2,4},{3,5},{4,2},{5,3},{6,0},{7,1},{8,14},{9,15},{10,... | collective-permute-start | bytes 884744 | tf_op jit(solution)/shard_map/backward_entry_chip3/ppermute | solution.py:288
  36.9 5.4 %collective-permute-start.8 = (bf16[4,48,384]{2,1,0:T(8,128)(2,1)S(1)}, bf16[4,48,384]{2,1,0:T(8,128)(2,1)S(1)}, u32[]{:S(2)}, u32[]{:S(2)}) collective-permute-start(bf16[4,48,384]{2,1,0:T(8,128)(2,1)S(1)} %pad_maximum_fusion.8.refs_1_), channel_id=1, source_target_pairs={{0,1},{1,0},{2,3},{3,2},{4,5},{5,4},{6,7},{7,6},{8,9},{9,8},{10,11... | collective-permute-start | bytes 442376 | tf_op jit(solution)/shard_map/mask_core/ppermute | solution.py:288
  41.8 28.7 %collective-permute-start.10 = (bf16[4,4,48,384]{3,2,1,0:T(8,128)(2,1)S(1)}, bf16[4,4,48,384]{3,2,1,0:T(8,128)(2,1)S(1)}, u32[]{:S(2)}, u32[]{:S(2)}) collective-permute-start(bf16[4,4,48,384]{3,2,1,0:T(8,128)(2,1)S(1)} %get-tuple-element.38), channel_id=1, source_target_pairs={{0,1},{1,0},{2,3},{3,2},{4,5},{5,4},{6,7},{7,6},{8,9},{9,8},{10,11... | collective-permute-start | bytes 1769480 | tf_op jit(solution)/shard_map/forward_exit_core/ppermute | solution.py:288
  62.7 7.8 %collective-permute-start.9 = (bf16[400,384]{1,0:T(8,128)(2,1)S(1)}, bf16[400,384]{1,0:T(8,128)(2,1)S(1)}, u32[]{:S(2)}, u32[]{:S(2)}) collective-permute-start(bf16[400,384]{1,0:T(8,128)(2,1)S(1)} %get-tuple-element.37), channel_id=1, source_target_pairs={{0,1},{1,0},{2,3},{3,2},{4,5},{5,4},{6,7},{7,6},{8,9},{9,8},{10,11... | collective-permute-start | bytes 921608 | tf_op jit(solution)/shard_map/over_core/ppermute | solution.py:288
  62.9 19.1 %collective-permute-start.14 = (bf16[4,48,384]{2,1,0:T(8,128)(2,1)S(1)}, bf16[4,48,384]{2,1,0:T(8,128)(2,1)S(1)}, u32[]{:S(2)}, u32[]{:S(2)}) collective-permute-start(bf16[4,48,384]{2,1,0:T(8,128)(2,1)S(1)} %get-tuple-element.53), channel_id=1, source_target_pairs={{0,4},{1,5},{2,6},{3,7},{4,0},{5,1},{6,2},{7,3},{8,12},{9,13},{10,... | collective-permute-start | bytes 442376 | tf_op jit(solution)/shard_map/forward_exit_start2/ppermute | solution.py:288
  70.6 11.4 %collective-permute-start.11 = (bf16[112,384]{1,0:T(8,128)(2,1)S(1)}, bf16[112,384]{1,0:T(8,128)(2,1)S(1)}, u32[]{:S(2)}, u32[]{:S(2)}) collective-permute-start(bf16[112,384]{1,0:T(8,128)(2,1)S(1)} %get-tuple-element.40), channel_id=1, source_target_pairs={{0,2},{1,3},{2,0},{3,1},{4,6},{5,7},{6,4},{7,5},{8,10},{9,11},{10,... | collective-permute-start | bytes 258056 | tf_op jit(solution)/shard_map/over_chip1/ppermute | solution.py:288
  71.0 12.8 %collective-permute-start.12 = (bf16[112,384]{1,0:T(8,128)(2,1)S(1)}, bf16[112,384]{1,0:T(8,128)(2,1)S(1)}, u32[]{:S(2)}, u32[]{:S(2)}) collective-permute-start(bf16[112,384]{1,0:T(8,128)(2,1)S(1)} %get-tuple-element.41), channel_id=1, source_target_pairs={{0,4},{1,5},{2,6},{3,7},{4,0},{5,1},{6,2},{7,3},{8,12},{9,13},{10,... | collective-permute-start | bytes 258056 | tf_op jit(solution)/shard_map/over_chip2/ppermute | solution.py:288
  72.6 11.2 %collective-permute-start.13 = (bf16[112,384]{1,0:T(8,128)(2,1)S(1)}, bf16[112,384]{1,0:T(8,128)(2,1)S(1)}, u32[]{:S(2)}, u32[]{:S(2)}) collective-permute-start(bf16[112,384]{1,0:T(8,128)(2,1)S(1)} %get-tuple-element.42), channel_id=1, source_target_pairs={{0,6},{1,7},{2,4},{3,5},{4,2},{5,3},{6,0},{7,1},{8,14},{9,15},{10,... | collective-permute-start | bytes 258056 | tf_op jit(solution)/shard_map/over_chip3/ppermute | solution.py:288
  84.4 6.9 %collective-permute-start.15 = (bf16[96,384]{1,0:T(8,128)(2,1)S(1)}, bf16[96,384]{1,0:T(8,128)(2,1)S(1)}, u32[]{:S(2)}, u32[]{:S(2)}) collective-permute-start(bf16[96,384]{1,0:T(8,128)(2,1)S(1)} %get-tuple-element.44.refs_0_), channel_id=1, source_target_pairs={{0,8},{8,0},{16,24},{24,16},{32,40},{40,32},{48,56},{56,48},{64,72... | collective-permute-start | bytes 221192 | tf_op jit(solution)/shard_map/over_x1/ppermute | solution.py:293
  85.9 15.0 %collective-permute-start.21 = (bf16[4,48,384]{2,1,0:T(8,128)(2,1)S(1)}, bf16[4,48,384]{2,1,0:T(8,128)(2,1)S(1)}, u32[]{:S(2)}, u32[]{:S(2)}) collective-permute-start(bf16[4,48,384]{2,1,0:T(8,128)(2,1)S(1)} %get-tuple-element.45), channel_id=1, source_target_pairs={{0,4},{1,5},{2,6},{3,7},{4,0},{5,1},{6,2},{7,3},{8,12},{9,13},{10,... | collective-permute-start | bytes 442376 | tf_op jit(solution)/shard_map/forward_exit_chip2/ppermute | solution.py:288
  88.0 5.9 %collective-permute-start.16 = (bf16[96,384]{1,0:T(8,128)(2,1)S(1)}, bf16[96,384]{1,0:T(8,128)(2,1)S(1)}, u32[]{:S(2)}, u32[]{:S(2)}) collective-permute-start(bf16[96,384]{1,0:T(8,128)(2,1)S(1)} %get-tuple-element.44.refs_0_), channel_id=1, source_target_pairs={{0,16},{8,24},{16,0},{24,8},{32,48},{40,56},{48,32},{56,40},{64,80... | collective-permute-start | bytes 221192 | tf_op jit(solution)/shard_map/over_x2/ppermute | solution.py:293
  90.7 5.6 %collective-permute-start.17 = (bf16[96,384]{1,0:T(8,128)(2,1)S(1)}, bf16[96,384]{1,0:T(8,128)(2,1)S(1)}, u32[]{:S(2)}, u32[]{:S(2)}) collective-permute-start(bf16[96,384]{1,0:T(8,128)(2,1)S(1)} %get-tuple-element.44.refs_0_), channel_id=1, source_target_pairs={{0,24},{8,16},{16,8},{24,0},{32,56},{40,48},{48,40},{56,32},{64,88... | collective-permute-start | bytes 221192 | tf_op jit(solution)/shard_map/over_x3/ppermute | solution.py:293
  91.2 24.2 %collective-permute-start.23 = (bf16[8,48,384]{2,1,0:T(8,128)(2,1)S(1)}, bf16[8,48,384]{2,1,0:T(8,128)(2,1)S(1)}, u32[]{:S(2)}, u32[]{:S(2)}) collective-permute-start(bf16[8,48,384]{2,1,0:T(8,128)(2,1)S(1)} %get-tuple-element.46), channel_id=1, source_target_pairs={{0,2},{1,3},{2,0},{3,1},{4,6},{5,7},{6,4},{7,5},{8,10},{9,11},{10,... | collective-permute-start | bytes 884744 | tf_op jit(solution)/shard_map/forward_exit_chip1/ppermute | solution.py:288
  91.3 24.1 %collective-permute-start.24 = (bf16[8,48,384]{2,1,0:T(8,128)(2,1)S(1)}, bf16[8,48,384]{2,1,0:T(8,128)(2,1)S(1)}, u32[]{:S(2)}, u32[]{:S(2)}) collective-permute-start(bf16[8,48,384]{2,1,0:T(8,128)(2,1)S(1)} %get-tuple-element.47), channel_id=1, source_target_pairs={{0,6},{1,7},{2,4},{3,5},{4,2},{5,3},{6,0},{7,1},{8,14},{9,15},{10,... | collective-permute-start | bytes 884744 | tf_op jit(solution)/shard_map/forward_exit_chip3/ppermute | solution.py:288
  96.3 4.9 %collective-permute-start.18 = (bf16[96,384]{1,0:T(8,128)(2,1)S(1)}, bf16[96,384]{1,0:T(8,128)(2,1)S(1)}, u32[]{:S(2)}, u32[]{:S(2)}) collective-permute-start(bf16[96,384]{1,0:T(8,128)(2,1)S(1)} %four_sum_kernel.2.refs_0_), channel_id=1, source_target_pairs={{0,64},{8,72},{16,80},{24,88},{32,96},{40,104},{48,112},{56,120},{... | collective-permute-start | bytes 221192 | tf_op jit(solution)/shard_map/over_y1/ppermute | solution.py:293
  98.0 6.0 %collective-permute-start.19 = (bf16[96,384]{1,0:T(8,128)(2,1)S(1)}, bf16[96,384]{1,0:T(8,128)(2,1)S(1)}, u32[]{:S(2)}, u32[]{:S(2)}) collective-permute-start(bf16[96,384]{1,0:T(8,128)(2,1)S(1)} %four_sum_kernel.2.refs_0_), channel_id=1, source_target_pairs={{0,128},{8,136},{16,144},{24,152},{32,160},{40,168},{48,176},{56,1... | collective-permute-start | bytes 221192 | tf_op jit(solution)/shard_map/over_y2/ppermute | solution.py:293
  100.9 5.6 %collective-permute-start.20 = (bf16[96,384]{1,0:T(8,128)(2,1)S(1)}, bf16[96,384]{1,0:T(8,128)(2,1)S(1)}, u32[]{:S(2)}, u32[]{:S(2)}) collective-permute-start(bf16[96,384]{1,0:T(8,128)(2,1)S(1)} %four_sum_kernel.2.refs_0_), channel_id=1, source_target_pairs={{0,192},{8,200},{16,208},{24,216},{32,224},{40,232},{48,240},{56,2... | collective-permute-start | bytes 221192 | tf_op jit(solution)/shard_map/over_y3/ppermute | solution.py:293
  106.5 8.9 %collective-permute-start.22 = (bf16[96,384]{1,0:T(8,128)(2,1)S(1)}, bf16[96,384]{1,0:T(8,128)(2,1)S(1)}, u32[]{:S(2)}, u32[]{:S(2)}) collective-permute-start(bf16[96,384]{1,0:T(8,128)(2,1)S(1)} %four_sum_kernel.3.refs_1_), channel_id=1, source_target_pairs={{0,32},{8,40},{16,48},{24,56},{32,0},{40,8},{48,16},{56,24},{64,96... | collective-permute-start | bytes 221192 | tf_op jit(solution)/shard_map/over_z/ppermute | solution.py:293
